TPU v7x, 256 devices: a whole 4x4x8 slice. The times are simulated.
256 devices in a mesh: angle: 4 (over y_lo, core), slab: 64 (over x, z, y_hi).
Axes of the slice: x: 4, y: 4 (y_hi: 2, y_lo: 2; y = y_hi * 2 + y_lo), z: 8, core: 2. Of those that a mesh axis runs over, the one named last changes fastest.
Arguments:
- coefficients: float32 [45, 128, 32, 128], P(None, 'slab'), may hold values from -6 to 6
- harmonics: float32 [8, 8, 45], P('angle'), may hold values from -0.875 to 0.875
- stretch: float32 [8], P('angle'), may hold values from 0.5 to 0.75
- measured: float32 [8, 8, 16384], P('angle', None, 'slab'), may hold values from -24 to 24
- tile_pixel: int32 [8, 12288], P('angle', 'slab'), may hold values from 0 to 127
- tile_voxel: int32 [8, 12288], P('angle', 'slab'), may hold values from 0 to 63
- tile_shift: float32 [8, 12288], P('angle', 'slab'), may hold values from 0 to 32
- tile_count: int32 [8, 64], P('angle', 'slab'), may hold values from 96 to 192, as said below
Outputs:
- updated: float32 [45, 128, 32, 128], P(None, 'slab')
- misfit: float32 [8, 8, 16384], P('angle', None, 'slab')
Inputs may be any that keep to these rules, and one draw needn't show every extreme that they name: `tile_voxel`: tile slots of slab d read voxel rows of slab d only. `tile_count`: every rotation has a slab with all 192 slots valid.
All inputs are finite; a program needn't handle non-finite values.
Results may differ from a plain program's by a relative error of at most 0.0001.
Values sent between devices are 32-bit elements; how exact they have to be, the bound alone decides.
A program may use at most 64 MiB of HBM per device.

v0:
```python
import jax
import jax.numpy as jnp
from jax import lax
from jax.sharding import PartitionSpec as P

ITERS = 2


tile_blocks = 4
step_size = 0.003
smoothing = 6.0


def padded_2(block, sides, width):
    for axis, dim in sides:
        count = lax.axis_size(axis)
        forward = [(i, i + 1) for i in range(count - 1)]
        backward = [(target, source) for source, target in forward]
        low = lax.ppermute(
            lax.slice_in_dim(block, block.shape[dim] - width, None, axis=dim), axis, forward
        )
        high = lax.ppermute(lax.slice_in_dim(block, 0, width, axis=dim), axis, backward)
        block = jnp.concatenate([low, block, high], axis=dim)
    return block


def footprint(shifts, stretch_value, width):
    position = jnp.arange(width).astype(shifts.dtype)
    offset = (
        position[None, None, :] - shifts[:, None, None] - stretch_value * position[None, :, None]
    )
    return jnp.maximum(0.0, 1.0 - jnp.abs(offset))


def project_rotation(
    seg_field, pixel_index, voxel_index, shifts, validity, stretch_value, pixel_tiles
):
    segments, voxel_rows, width = seg_field.shape
    per_block = shifts.shape[0] // tile_blocks

    def project_accumulate(total, inputs_block):
        block_pixels, block_voxels, block_shifts, block_valid = inputs_block
        weights = footprint(block_shifts, stretch_value, width) * block_valid[:, None, None]
        picked = seg_field[:, block_voxels, :]
        contrib = jnp.einsum("stv,tvp->tsp", picked, weights, precision=lax.Precision.HIGHEST)
        return (total.at[block_pixels].add(contrib), None)

    inputs_all = tuple(
        (
            entry.reshape(tile_blocks, per_block)
            for entry in (pixel_index, voxel_index, shifts, validity)
        )
    )
    total, unused = lax.scan(
        project_accumulate, jnp.zeros((pixel_tiles, segments, width), jnp.float32), inputs_all
    )
    return total.transpose(1, 0, 2).reshape(segments, pixel_tiles * width)


def back_rotation(
    misfit_rows, pixel_index, voxel_index, shifts, validity, stretch_value, voxel_rows
):
    segments, pixel_tiles, width = misfit_rows.shape
    per_block = shifts.shape[0] // tile_blocks

    def back_accumulate(total, inputs_block):
        block_pixels, block_voxels, block_shifts, block_valid = inputs_block
        weights = footprint(block_shifts, stretch_value, width) * block_valid[:, None, None]
        picked = misfit_rows[:, block_pixels, :]
        contrib = jnp.einsum("stp,tvp->tsv", picked, weights, precision=lax.Precision.HIGHEST)
        return (total.at[block_voxels].add(contrib), None)

    inputs_all = tuple(
        (
            entry.reshape(tile_blocks, per_block)
            for entry in (pixel_index, voxel_index, shifts, validity)
        )
    )
    total, unused = lax.scan(
        back_accumulate, jnp.zeros((voxel_rows, segments, width), jnp.float32), inputs_all
    )
    return total.transpose(1, 0, 2)


def yx_neighbours(field):
    padded = jnp.pad(field, ((0, 0), (0, 0), (1, 1), (1, 1)))
    return (
        padded[:, :, 2:, 1:-1]
        + padded[:, :, :-2, 1:-1]
        + padded[:, :, 1:-1, 2:]
        + padded[:, :, 1:-1, :-2]
    )


def per_device(
    coefficients, harmonics, stretch, measured, tile_pixel, tile_voxel, tile_shift, tile_count
):
    channels, depth, height, width = coefficients.shape
    voxel_rows = depth * height
    rotations, segments, share = measured.shape
    pixels = share * lax.axis_size("slab")
    pixel_tiles = pixels // width
    validity = (jnp.arange(tile_pixel.shape[1])[None, :] < tile_count).astype(jnp.float32)
    coeffs = coefficients
    misfit = measured
    for iteration in range(ITERS):
        padded = padded_2(coeffs, (("slab", 1),), 1)
        laplace = 6.0 * coeffs - padded[:, 2:] - padded[:, :-2] - yx_neighbours(coeffs)
        flat = coeffs.reshape(channels, voxel_rows, width)
        partials = []
        for rotation in range(rotations):
            seg_field = jnp.einsum(
                "sk,kqx->sqx", harmonics[rotation], flat, precision=lax.Precision.HIGHEST
            )
            partials.append(
                project_rotation(
                    seg_field,
                    tile_pixel[rotation],
                    tile_voxel[rotation],
                    tile_shift[rotation],
                    validity[rotation],
                    stretch[rotation],
                    pixel_tiles,
                )
            )
        partial_sums = jnp.stack(partials)
        misfit = lax.psum_scatter(partial_sums, "slab", scatter_dimension=2, tiled=True) - measured
        whole_misfit = lax.all_gather(misfit, "slab", axis=2, tiled=True)
        backs = []
        for rotation in range(rotations):
            misfit_rows = whole_misfit[rotation].reshape(segments, pixel_tiles, width)
            backs.append(
                back_rotation(
                    misfit_rows,
                    tile_pixel[rotation],
                    tile_voxel[rotation],
                    tile_shift[rotation],
                    validity[rotation],
                    stretch[rotation],
                    voxel_rows,
                )
            )
        back_all = jnp.stack(backs)
        local_terms = jnp.einsum(
            "rsk,rsqx->kqx", harmonics, back_all, precision=lax.Precision.HIGHEST
        )
        gradient = lax.psum(local_terms, "angle")
        coeffs = coeffs - step_size * (gradient.reshape(coeffs.shape) + smoothing * laplace)
    return (coeffs, misfit)


def solution(mesh):
    in_specs = (
        P(None, "slab", None, None),
        P("angle", None, None),
        P("angle"),
        P("angle", None, "slab"),
        P("angle", "slab"),
        P("angle", "slab"),
        P("angle", "slab"),
        P("angle", "slab"),
    )
    out_specs = (P(None, "slab", None, None), P("angle", None, "slab"))
    return jax.shard_map(
        per_device, mesh=mesh, in_specs=in_specs, out_specs=out_specs, check_vma=False
    )
```

profile of v0, /device:TPU:1, one launch (start us, length us, event | category | flops | bytes accessed | tf_op | source)
XLA Modules:
  0.0 1357.8 jit_solution(16570831156897262543)
XLA Ops:
  13.2 26.2 %while.80 = (s32[]{:T(128)}, f32[128,8,128]{2,1,0:T(8,128)S(1)}, s32[4,48]{1,0:T(4,128)S(1)}, s32[4,48]{1,0:T(4,128)S(1)}, f32[8,64,128]{2,0,1:T(8,128)S(1)}, /*...) while((s32[]{:T(128)}, f32[128,8,128]{2,1,0:T(8,128)S(1)}, s32[4,48]{1,0:T(4,128)S(1)}, ...), condition=%wide.region_2.3_spmd, body=%wide.region_0.2_spmd.sunk | while | flops 79486624 | bytes 1434153 | solution.py:54
  39.8 26.5 %while.81 = (s32[]{:T(128)}, f32[128,8,128]{2,1,0:T(8,128)S(1)}, s32[4,48]{1,0:T(4,128)S(1)}, s32[4,48]{1,0:T(4,128)S(1)}, f32[8,64,128]{2,0,1:T(8,128)S(1)}, /*...) while((s32[]{:T(128)}, f32[128,8,128]{2,1,0:T(8,128)S(1)}, s32[4,48]{1,0:T(4,128)S(1)}, ...), condition=%wide.region_5.6_spmd, body=%wide.region_3.5_spmd.sunk | while | flops 79486624 | bytes 1434153 | solution.py:54
  67.5 315.8 %reduce-scatter.3.cloned.1.call-done = f32[2,8,256]{2,1,0:T(8,128)} async-done(((f32[2,8,16384]{2,1,0:T(8,128)}), f32[2,8,256]{2,1,0:T(8,128)}) %reduce-scatter.3.cloned.1.call-update) | async-done | bytes 16400 | tf_op jit(solution)/shard_map/reduce_scatter | solution.py:127
  384.8 148.0 %all-gather.3.cloned.1.call-done = f32[2,8,16384]{2,1,0:T(8,128)} async-done(((f32[2,8,256]{2,1,0:T(8,128)}), f32[2,8,16384]{2,1,0:T(8,128)}) %all-gather.3.cloned.1.call-update) | async-done | bytes 1048592 | tf_op jit(solution)/shard_map/all_gather | solution.py:128
  534.1 34.6 %while.82 = (s32[]{:T(128)}, f32[64,8,128]{2,1,0:T(8,128)S(1)}, s32[4,48]{1,0:T(4,128)S(1)}, s32[4,48]{1,0:T(4,128)S(1)}, f32[8,128,128]{2,0,1:T(8,128)S(1)}, /*...) while((s32[]{:T(128)}, f32[64,8,128]{2,1,0:T(8,128)S(1)}, s32[4,48]{1,0:T(4,128)S(1)}, ...), condition=%wide.region_9.10_spmd, body=%wide.region_7.9_spmd.sunk | while | flops 79486624 | bytes 1434153 | solution.py:79
  535.5 5.1 fusion.271
  544.1 5.1 fusion.271
  552.8 5.1 fusion.271
  561.4 5.1 fusion.271
  568.8 34.8 %while.83 = (s32[]{:T(128)}, f32[64,8,128]{2,1,0:T(8,128)S(1)}, s32[4,48]{1,0:T(4,128)S(1)}, s32[4,48]{1,0:T(4,128)S(1)}, f32[8,128,128]{2,0,1:T(8,128)S(1)}, /*...) while((s32[]{:T(128)}, f32[64,8,128]{2,1,0:T(8,128)S(1)}, ...), condition=%wide.region_12.13_spmd, body=%wide.region_10.12_spmd.sunk | while | flops 79486624 | bytes 1434153 | solution.py:79
  570.2 5.1 fusion.276
  578.9 5.1 fusion.276
  587.6 5.1 fusion.276
  596.3 5.1 fusion.276
  609.2 5.7 collective-permute-start.1
  615.0 13.7 %collective-permute-done = f32[45,1,32,128]{3,2,1,0:T(8,128)S(1)} collective-permute-done((f32[45,1,32,128]{3,2,1,0:T(8,128)}, f32[45,1,32,128]{3,2,1,0:T(8,128)S(1)}, u32[]{:S(2)}, u32[]{:S(2)}) %collective-permute-start) | collective-permute-done | bytes 737312 | tf_op jit(solution)/shard_map/ppermute | solution.py:22
  628.7 26.9 %collective-permute-done.1 = f32[45,1,32,128]{3,2,1,0:T(8,128)S(1)} collective-permute-done((f32[45,1,32,128]{3,2,1,0:T(8,128)}, f32[45,1,32,128]{3,2,1,0:T(8,128)S(1)}, u32[]{:S(2)}, u32[]{:S(2)}) %collective-permute-start.1) | collective-permute-done | bytes 737312 | tf_op jit(solution)/shard_map/ppermute | solution.py:19
  656.5 23.0 %all-reduce.5.cloned.1.call-done = f32[45,2,32,128]{3,2,1,0:T(8,128)} async-done(((f32[45,2,32,128]{3,2,1,0:T(8,128)}), f32[45,2,32,128]{3,2,1,0:T(8,128)}) %all-reduce.5.cloned.1.call-update) | async-done | bytes 1474576 | tf_op jit(solution)/shard_map/psum | solution.py:147
  686.3 26.2 %while.84 = (s32[]{:T(128)}, f32[128,8,128]{2,1,0:T(8,128)S(1)}, s32[4,48]{1,0:T(4,128)S(1)}, s32[4,48]{1,0:T(4,128)S(1)}, f32[8,64,128]{2,0,1:T(8,128)S(1)}, /*...) while((s32[]{:T(128)}, f32[128,8,128]{2,1,0:T(8,128)S(1)}, ...), condition=%wide.region_16.17_spmd, body=%wide.region_14.16_spmd.sunk | while | flops 79486624 | bytes 1434153 | solution.py:54
  712.6 26.5 %while.85 = (s32[]{:T(128)}, f32[128,8,128]{2,1,0:T(8,128)S(1)}, s32[4,48]{1,0:T(4,128)S(1)}, s32[4,48]{1,0:T(4,128)S(1)}, f32[8,64,128]{2,0,1:T(8,128)S(1)}, /*...) while((s32[]{:T(128)}, f32[128,8,128]{2,1,0:T(8,128)S(1)}, ...), condition=%wide.region_19.20_spmd, body=%wide.region_17.19_spmd.sunk | while | flops 79486624 | bytes 1434153 | solution.py:54
  740.2 313.0 %reduce-scatter.5.cloned.1.call-done = f32[2,8,256]{2,1,0:T(8,128)} async-done(((f32[2,8,16384]{2,1,0:T(8,128)}), f32[2,8,256]{2,1,0:T(8,128)}) %reduce-scatter.5.cloned.1.call-update) | async-done | bytes 16400 | tf_op jit(solution)/shard_map/reduce_scatter | solution.py:127
  1054.9 146.7 %all-gather.5.cloned.1.call-done = f32[2,8,16384]{2,1,0:T(8,128)} async-done(((f32[2,8,256]{2,1,0:T(8,128)}), f32[2,8,16384]{2,1,0:T(8,128)}) %all-gather.5.cloned.1.call-update) | async-done | bytes 1048592 | tf_op jit(solution)/shard_map/all_gather | solution.py:128
  1202.8 34.6 %while.86 = (s32[]{:T(128)}, f32[64,8,128]{2,1,0:T(8,128)S(1)}, s32[4,48]{1,0:T(4,128)S(1)}, s32[4,48]{1,0:T(4,128)S(1)}, f32[8,128,128]{2,0,1:T(8,128)S(1)}, /*...) while((s32[]{:T(128)}, f32[64,8,128]{2,1,0:T(8,128)S(1)}, ...), condition=%wide.region_23.24_spmd, body=%wide.region_21.23_spmd.sunk | while | flops 79486624 | bytes 1434153 | solution.py:79
  1204.2 5.1 fusion.291
  1212.8 5.1 fusion.291
  1221.5 5.1 fusion.291
  1230.1 5.1 fusion.291
  1237.5 34.8 %while.87 = (s32[]{:T(128)}, f32[64,8,128]{2,1,0:T(8,128)S(1)}, s32[4,48]{1,0:T(4,128)S(1)}, s32[4,48]{1,0:T(4,128)S(1)}, f32[8,128,128]{2,0,1:T(8,128)S(1)}, /*...) while((s32[]{:T(128)}, f32[64,8,128]{2,1,0:T(8,128)S(1)}, ...), condition=%wide.region_26.27_spmd, body=%wide.region_24.26_spmd.sunk | while | flops 79486624 | bytes 1434153 | solution.py:79
  1276.8 5.5 collective-permute-start.3
  1282.3 12.3 collective-permute-done.2
  1294.7 28.2 %collective-permute-done.3 = f32[45,1,32,128]{3,2,1,0:T(8,128)S(1)} collective-permute-done((f32[45,1,32,128]{3,2,1,0:T(8,128)S(1)}, f32[45,1,32,128]{3,2,1,0:T(8,128)S(1)}, u32[]{:S(2)}, u32[]{:S(2)}) %collective-permute-start.3) | collective-permute-done | bytes 737312 | tf_op jit(solution)/shard_map/ppermute | solution.py:19
  1322.9 24.0 %all-reduce.7.cloned.1.call-done = f32[45,2,32,128]{3,2,1,0:T(8,128)} async-done(((f32[45,2,32,128]{3,2,1,0:T(8,128)}), f32[45,2,32,128]{3,2,1,0:T(8,128)}) %all-reduce.7.cloned.1.call-update) | async-done | bytes 1474576 | tf_op jit(solution)/shard_map/psum | solution.py:147
  (348 shorter events, 216.6 us)
Async XLA Ops:
  7.2 3.2 copy-start
  7.2 3.2 copy-start.3
  7.2 376.0 %reduce-scatter.3.cloned.1.call-start = ((), (), s32[]{:S(2)}) async-start(), calls=%async_computation.2 | async-start | bytes 1064960 | tf_op jit(solution)/shard_map/reduce_scatter | solution.py:127
  7.2 4.8 copy-start.9
  7.2 4.9 copy-start.6
  7.3 5.1 copy-start.7
  7.3 5.1 copy-start.8
  7.3 5.3 copy-start.5
  66.3 316.9 %copy-start.4 = (f32[2,8,256]{2,1,0:T(8,128)S(1)}, f32[2,8,256]{2,1,0:T(8,128)}, u32[]{:S(2)}) copy-start(f32[2,8,256]{2,1,0:T(8,128)} %param.27) | copy-start | bytes 49156
  67.4 465.4 %all-gather.3.cloned.1.call-start = ((), (), s32[]{:S(2)}) async-start(), calls=%async_computation.3 | async-start | bytes 1064960 | tf_op jit(solution)/shard_map/all_gather | solution.py:128
  384.6 294.9 %all-reduce.5.cloned.1.call-start = ((), (), s32[]{:S(2)}) async-start(), calls=%async_computation.4 | async-start | bytes 2949120 | tf_op jit(solution)/shard_map/psum | solution.py:147
  606.6 446.6 %reduce-scatter.5.cloned.1.call-start = ((), (), s32[]{:S(2)}) async-start(), calls=%async_computation.5 | async-start | bytes 1064960 | tf_op jit(solution)/shard_map/reduce_scatter | solution.py:127
  607.9 20.8 %collective-permute-start = (f32[45,1,32,128]{3,2,1,0:T(8,128)}, f32[45,1,32,128]{3,2,1,0:T(8,128)S(1)}, u32[]{:S(2)}, u32[]{:S(2)}) collective-permute-start(f32[45,1,32,128]{3,2,1,0:T(8,128)} %get-tuple-element.564), channel_id=1, source_target_pairs={{1,0},{2,1},{3,2},{4,3},{5,4},{6,5},{7,6},{8,7},{9,8},{10,9},{11,1... | collective-permute-start | bytes 2211848 | tf_op jit(solution)/shard_map/ppermute | solution.py:22
  609.2 46.4 %collective-permute-start.1 = (f32[45,1,32,128]{3,2,1,0:T(8,128)}, f32[45,1,32,128]{3,2,1,0:T(8,128)S(1)}, u32[]{:S(2)}, u32[]{:S(2)}) collective-permute-start(f32[45,1,32,128]{3,2,1,0:T(8,128)} %get-tuple-element.565), channel_id=1, source_target_pairs={{0,1},{1,2},{2,3},{3,4},{4,5},{5,6},{6,7},{7,8},{8,9},{9,10},{10,1... | collective-permute-start | bytes 2211848 | tf_op jit(solution)/shard_map/ppermute | solution.py:19
  628.7 26.9 %copy-start.1 = (f32[45,1,32,128]{3,2,1,0:T(8,128)}, f32[45,1,32,128]{3,2,1,0:T(8,128)S(1)}, u32[]{:S(2)}) copy-start(f32[45,1,32,128]{3,2,1,0:T(8,128)S(1)} %collective-permute-done) | copy-start | bytes 2211844
  655.6 0.9 copy-start.2
  740.1 461.4 %all-gather.5.cloned.1.call-start = ((), (), s32[]{:S(2)}) async-start(), calls=%async_computation.6 | async-start | bytes 1064960 | tf_op jit(solution)/shard_map/all_gather | solution.py:128
  1054.6 292.3 %all-reduce.7.cloned.1.call-start = ((), (), s32[]{:S(2)}) async-start(), calls=%async_computation.7 | async-start | bytes 2949120 | tf_op jit(solution)/shard_map/psum | solution.py:147
  1275.5 19.2 %collective-permute-start.2 = (f32[45,1,32,128]{3,2,1,0:T(8,128)S(1)}, f32[45,1,32,128]{3,2,1,0:T(8,128)S(1)}, u32[]{:S(2)}, u32[]{:S(2)}) collective-permute-start(f32[45,1,32,128]{3,2,1,0:T(8,128)S(1)} %get-tuple-element.562), channel_id=1, source_target_pairs={{1,0},{2,1},{3,2},{4,3},{5,4},{6,5},{7,6},{8,7},{9,8},{10,9},{11,1... | collective-permute-start | bytes 2211848 | tf_op jit(solution)/shard_map/ppermute | solution.py:22
  1276.8 46.1 %collective-permute-start.3 = (f32[45,1,32,128]{3,2,1,0:T(8,128)S(1)}, f32[45,1,32,128]{3,2,1,0:T(8,128)S(1)}, u32[]{:S(2)}, u32[]{:S(2)}) collective-permute-start(f32[45,1,32,128]{3,2,1,0:T(8,128)S(1)} %get-tuple-element.563), channel_id=1, source_target_pairs={{0,1},{1,2},{2,3},{3,4},{4,5},{5,6},{6,7},{7,8},{8,9},{9,10},{10,1... | collective-permute-start | bytes 2211848 | tf_op jit(solution)/shard_map/ppermute | solution.py:19
Sparse Core Ops, SparseCore 0:
  67.5 315.6 reduce-scatter.2
  387.8 144.9 all-gather.2
  606.7 72.7 all-reduce.4
  740.3 312.9 reduce-scatter.4
  1057.7 143.8 all-gather.4
  1275.5 71.3 all-reduce.6
where the time goes:
time: 1370 us; the launch traced here: 1360 us
  waiting for transfers between devices  1050 us (77%)
  matrix products  141 us (10%)
  other arithmetic  104 us (8%)
  local copies, waits for them, and re-layouts  29.3 us (2%)
  between operations  14.9 us (1%)
  starting transfers between devices  14.5 us (1%)
    reduce_scatter x2, waiting for transfers between devices, per_device(): lax.psum_scatter(partial_sums, 'slab', scatter_dimension=2, tiled=True)  629 us
    all_gather x2, waiting for transfers between devices, per_device(): whole_misfit = lax.all_gather(misfit, 'slab', axis=2, tiled=True)  295 us
    dot_general x16, matrix products, back_accumulate(): jnp.einsum('stp,tvp->tsv', picked, weights, precision=lax.Precision.HIGHEST)  81.7 us
    ppermute x2, waiting for transfers between devices, padded_2(): lax.ppermute(lax.slice_in_dim(block, block.shape[dim] - width, None, axis...  55.2 us
    dot_general x16, matrix products, project_accumulate(): jnp.einsum('stv,tvp->tsp', picked, weights, precision=lax.Precision.HIGHEST)  48.5 us
    psum x2, waiting for transfers between devices, per_device(): gradient = lax.psum(local_terms, 'angle')  47 us
    scatter-add x16, other arithmetic, back_accumulate(): return (total.at[block_voxels].add(contrib), None)  35.2 us
    scatter-add x16, other arithmetic, project_accumulate(): return (total.at[block_pixels].add(contrib), None)  35 us
  transfers between devices with their start and end apart: 10, of which 10 were waited for; matrix products, arithmetic and copies ran while one was open for 0% of the time, Pallas kernels for 0%

commit v1 on v0

v1 whole, which is shorter than its diff:
```python
import jax
import jax.numpy as jnp
from jax import lax
from jax.experimental import pallas as pl
from jax.experimental.pallas import tpu as pltpu
from jax.sharding import PartitionSpec as P

f32 = jnp.float32
MESH = pl.DeviceIdType.MESH
STEP = 0.003
SMOOTH = 6.0
NA = 2
FAR = 1.0e6

VM = pl.BlockSpec(memory_space=pltpu.VMEM)
SM = pl.BlockSpec(memory_space=pltpu.SMEM)
LIMIT = 48 * 2**20


def position():
    angle = lax.axis_index("angle")
    slab = lax.axis_index("slab")
    return angle, lax.div(slab, 16), lax.rem(lax.div(slab, 2), 8), lax.rem(slab, 2)


def device(angle, x, z, half):
    return (angle, (x * 8 + z) * 2 + half)


def greet(partners):
    barrier = pltpu.get_barrier_semaphore()
    for partner in partners:
        pl.semaphore_signal(barrier, inc=1, device_id=partner, device_id_type=MESH)
    pl.semaphore_wait(barrier, len(partners))


def send(src, dst, send_sem, recv_sem, target):
    copy = pltpu.make_async_remote_copy(
        src_ref=src, dst_ref=dst, send_sem=send_sem, recv_sem=recv_sem, device_id=target, device_id_type=MESH
    )
    copy.start()
    return copy


def dot(a, b):
    return jnp.dot(a, b, preferred_element_type=f32, precision=lax.Precision.HIGHEST)


def begin_kernel(c_ref, harm_ref, pack_ref, meas_ref, field_ref, harm_all_ref, pack_got, meas_got, out_ref, send_sem, recv_sem):
    angle, x, z, half = position()
    other = 1 - half
    partner = device(angle, x, z, other)
    peers = [device(lax.rem(angle + k, 4), x, z, half) for k in range(1, 4)]
    greet([partner] + peers)
    copies = [
        send(pack_ref, pack_got, send_sem.at[0], recv_sem.at[0], partner),
        send(meas_ref, meas_got, send_sem.at[1], recv_sem.at[1], partner),
    ]
    for k, peer in enumerate(peers):
        copies.append(send(harm_ref, harm_all_ref.at[angle], send_sem.at[2 + k], recv_sem.at[2 + k], peer))
    harm_all_ref[angle] = harm_ref[...]

    def fields(which, dest, base):
        rows = harm_ref[pl.ds(pl.multiple_of(which * 8, 8), 8), :][:, :48]
        for chunk in range(4):
            out = dot(rows, c_ref[chunk])
            for row in range(16):
                dest[base + chunk * 16 + row] = out[:, row * 128 : row * 128 + 128]

    fields(other, out_ref, 0)
    copies.append(send(out_ref, field_ref.at[pl.ds(64, 64)], send_sem.at[5], recv_sem.at[5], partner))
    fields(half, field_ref, 0)
    for copy in copies:
        copy.wait()


def begin(c_all, harm, pack, measured):
    return pl.pallas_call(
        begin_kernel,
        out_shape=(
            jax.ShapeDtypeStruct((128, 8, 128), f32),
            jax.ShapeDtypeStruct((4, 16, 128), f32),
            jax.ShapeDtypeStruct(pack.shape, f32),
            jax.ShapeDtypeStruct(measured.shape, f32),
        ),
        in_specs=[VM] * 4,
        out_specs=(VM,) * 4,
        scratch_shapes=[pltpu.VMEM((64, 8, 128), f32), pltpu.SemaphoreType.DMA((6,)), pltpu.SemaphoreType.DMA((6,))],
        compiler_params=pltpu.CompilerParams(collective_id=0, has_side_effects=True, vmem_limit_bytes=LIMIT),
        name="begin",
    )(c_all, harm, pack, measured)


def project_kernel(stretch_ref, slot_ref, shift_ref, field_ref, proj_ref, w_ref, i_ref):
    a = stretch_ref[0]
    inv = stretch_ref[1]
    lane = lax.broadcasted_iota(jnp.int32, (8, 128), 1).astype(f32)
    groups = shift_ref.shape[0]

    def weights(g, carry):
        u = lane - shift_ref[g]
        v0 = jnp.floor((u - 1.0) * inv) + 1.0
        t0 = u - a * v0
        taps = (1.0 - t0, 1.0 - jnp.abs(t0 - a), 1.0 + t0 - 2.0 * a, 1.0 + t0 - 3.0 * a)
        for j, w in enumerate(taps):
            v = v0 + float(j)
            w_ref[g, j] = jnp.where((v >= 0.0) & (v <= 127.0), jnp.maximum(w, 0.0), 0.0)
        i_ref[g] = v0.astype(jnp.int32)
        return carry

    lax.fori_loop(0, groups, weights, 0)
    proj_ref[...] = jnp.zeros_like(proj_ref)

    def slots(g, carry):
        sums = []
        for j in range(8):
            f = field_ref[slot_ref[1, g * 8 + j]]
            i0 = jnp.broadcast_to(i_ref[g, j : j + 1, :], (8, 128))
            parts = []
            for k in range(4):
                w = jnp.broadcast_to(w_ref[g, k, j : j + 1, :], (8, 128))
                parts.append(jnp.take_along_axis(f, (i0 + k) & 127, axis=1, mode="promise_in_bounds") * w)
            sums.append((parts[0] + parts[1]) + (parts[2] + parts[3]))
        for j in range(8):
            p = slot_ref[0, g * 8 + j]
            proj_ref[p] = proj_ref[p] + sums[j]
        return carry

    lax.fori_loop(0, groups, slots, 0)


def back_kernel(stretch_ref, slot_ref, shift_ref, misfit_ref, back_ref, w_ref, i_ref):
    a = stretch_ref[0]
    lane = lax.broadcasted_iota(jnp.int32, (8, 128), 1).astype(f32)
    groups = shift_ref.shape[0]

    def weights(g, carry):
        t = shift_ref[g] + a * lane
        p0 = jnp.floor(t)
        w1 = t - p0
        w_ref[g, 0] = jnp.where(p0 <= 127.0, 1.0 - w1, 0.0)
        w_ref[g, 1] = jnp.where(p0 <= 126.0, w1, 0.0)
        i_ref[g] = p0.astype(jnp.int32)
        return carry

    lax.fori_loop(0, groups, weights, 0)
    back_ref[...] = jnp.zeros_like(back_ref)

    def slots(g, carry):
        sums = []
        for j in range(8):
            m = misfit_ref[slot_ref[0, g * 8 + j]]
            i0 = jnp.broadcast_to(i_ref[g, j : j + 1, :], (8, 128))
            parts = []
            for k in range(2):
                w = jnp.broadcast_to(w_ref[g, k, j : j + 1, :], (8, 128))
                parts.append(jnp.take_along_axis(m, (i0 + k) & 127, axis=1, mode="promise_in_bounds") * w)
            sums.append(parts[0] + parts[1])
        for j in range(8):
            q = slot_ref[1, g * 8 + j]
            back_ref[q] = back_ref[q] + sums[j]
        return carry

    lax.fori_loop(0, groups, slots, 0)


def rays(body, taps, name, stretch2, slots, shifts, rows):
    groups = shifts.shape[0]
    return pl.pallas_call(
        body,
        out_shape=jax.ShapeDtypeStruct((128, 8, 128), f32),
        in_specs=[SM, SM, VM, VM],
        out_specs=VM,
        scratch_shapes=[pltpu.VMEM((groups, taps, 8, 128), f32), pltpu.VMEM((groups, 8, 128), jnp.int32)],
        compiler_params=pltpu.CompilerParams(vmem_limit_bytes=LIMIT),
        name=name,
    )(stretch2, slots, shifts, rows)


def reduce_kernel(
    proj_ref, meas_ref, c_ref,
    mis_ref, own_ref, zlow_ref, zhigh_ref, ylow_ref, yhigh_ref,
    a1, b1, a2, b2, sum_a, sum_b, send_sem, recv_sem,
):
    angle, x, z, half = position()
    slab = (x * 8 + z) * 2 + half
    nb = 4 - NA
    part_a, part_b = pl.ds(0, NA), pl.ds(NA, nb)
    xs = [lax.rem(x + k, 4) for k in range(1, 4)]
    zs = [lax.rem(z + k, 8) for k in range(1, 8)]
    to_x = [device(angle, xx, z, half) for xx in xs]
    to_z = [device(angle, x, zz, half) for zz in zs]
    above = (angle, lax.rem(slab + 1, 64))
    below = (angle, lax.rem(slab + 63, 64))
    right = (lax.rem(angle + 1, 4), slab)
    left = (lax.rem(angle + 3, 4), slab)
    greet(to_x + to_z + [above, below, right, left])

    count = [0]

    def put(src, dst, target):
        k = count[0]
        count[0] += 1
        return send(src, dst, send_sem.at[k], recv_sem.at[k], target)

    first_b = [put(proj_ref.at[:, zs[k], part_b], b1.at[k], to_z[k]) for k in range(7)]
    first_a = [put(proj_ref.at[xs[k], :, part_a], a1.at[k], to_x[k]) for k in range(3)]
    halos = [
        put(c_ref.at[:, pl.ds(1024, 1024)], zlow_ref, above),
        put(c_ref.at[:, pl.ds(0, 1024)], zhigh_ref, below),
    ]
    for s in range(2):
        halos.append(put(c_ref.at[:, pl.ds(s * 1024 + 896, 128)], ylow_ref.at[:, pl.ds(s * 128, 128)], right))
        halos.append(put(c_ref.at[:, pl.ds(s * 1024, 128)], yhigh_ref.at[:, pl.ds(s * 128, 128)], left))

    for copy in first_a:
        copy.wait_recv()
    sum_a[...] = proj_ref[x, :, :NA] + a1[0] + a1[1] + a1[2]
    second_a = [put(sum_a.at[zs[k]], a2.at[k], to_z[k]) for k in range(7)]
    for copy in first_b:
        copy.wait_recv()
    sum_b[...] = proj_ref[:, z, NA:] + ((b1[0] + b1[1]) + (b1[2] + b1[3])) + ((b1[4] + b1[5]) + b1[6])
    second_b = [put(sum_b.at[xs[k]], b2.at[k], to_x[k]) for k in range(3)]
    for copy in second_a:
        copy.wait_recv()
    total_a = sum_a[z] + ((a2[0] + a2[1]) + (a2[2] + a2[3])) + ((a2[4] + a2[5]) + a2[6]) - meas_ref[:NA]
    own_ref[:NA] = total_a
    mis_ref[x, z, :NA] = total_a
    third_a = [put(own_ref.at[part_a], mis_ref.at[x, z, part_a], to_z[k]) for k in range(7)]
    for copy in second_b:
        copy.wait_recv()
    total_b = sum_b[x] + (b2[0] + b2[1]) + b2[2] - meas_ref[NA:]
    own_ref[NA:] = total_b
    mis_ref[x, z, NA:] = total_b
    third_b = [put(own_ref.at[part_b], mis_ref.at[x, z, part_b], to_x[k]) for k in range(3)]
    for copy in third_b:
        copy.wait_recv()
    fourth_b = [put(mis_ref.at[:, z, part_b], mis_ref.at[:, z, part_b], to_z[k]) for k in range(7)]
    for copy in third_a:
        copy.wait_recv()
    fourth_a = [put(mis_ref.at[x, :, part_a], mis_ref.at[x, :, part_a], to_x[k]) for k in range(3)]
    for copy in fourth_a + fourth_b:
        copy.wait_recv()
    for copy in halos:
        copy.wait_recv()
    for copy in first_a + first_b + second_a + second_b + third_a + third_b + fourth_a + fourth_b + halos:
        copy.wait_send()


def reduce(proj, measured, c_own):
    nb = 4 - NA
    return pl.pallas_call(
        reduce_kernel,
        out_shape=(
            jax.ShapeDtypeStruct((4, 8, 4, 8, 128), f32),
            jax.ShapeDtypeStruct((4, 8, 128), f32),
            jax.ShapeDtypeStruct((48, 1024), f32),
            jax.ShapeDtypeStruct((48, 1024), f32),
            jax.ShapeDtypeStruct((48, 256), f32),
            jax.ShapeDtypeStruct((48, 256), f32),
        ),
        in_specs=[VM] * 3,
        out_specs=(VM,) * 6,
        scratch_shapes=[
            pltpu.VMEM((3, 8, NA, 8, 128), f32),
            pltpu.VMEM((7, 4, nb, 8, 128), f32),
            pltpu.VMEM((7, NA, 8, 128), f32),
            pltpu.VMEM((3, nb, 8, 128), f32),
            pltpu.VMEM((8, NA, 8, 128), f32),
            pltpu.VMEM((4, nb, 8, 128), f32),
            pltpu.SemaphoreType.DMA((46,)),
            pltpu.SemaphoreType.DMA((46,)),
        ],
        compiler_params=pltpu.CompilerParams(collective_id=1, has_side_effects=True, vmem_limit_bytes=LIMIT),
        name="reduce",
    )(proj, measured, c_own)


def column_partners(angle, x, z, half):
    found = []
    for k in range(1, 8):
        ta, th = lax.rem(angle + k // 2, 4), lax.rem(half + k % 2, 2)
        found.append((k, ta, th, device(ta, x, z, th)))
    return found


def send_back(back_ref, got, rotation, partners, send_sem, recv_sem):
    copies = []
    for k, ta, th, target in partners:
        src = back_ref.at[pl.ds(pl.multiple_of((k % 2) * 64 + ta * 16, 16), 16)]
        copies.append(send(src, got.at[rotation], send_sem.at[k - 1], recv_sem.at[k - 1], target))
    return copies


def smooth(angle, slab, c_ref, zlow_ref, zhigh_ref, ylow_ref, yhigh_ref, next_ref):
    lane = lax.broadcasted_iota(jnp.int32, (48, 128), 1)
    has_zlow = (slab > 0).astype(f32)
    has_zhigh = (slab < 63).astype(f32)
    has_ylow = (angle > 0).astype(f32)
    has_yhigh = (angle < 3).astype(f32)

    def at(ref, row):
        return ref[:, row * 128 : row * 128 + 128]

    for s in range(2):
        for y in range(8):
            row = s * 8 + y
            c = at(c_ref, row)
            near = at(zlow_ref, y) * has_zlow + at(c_ref, y + 8) if s == 0 else at(c_ref, y) + at(zhigh_ref, y) * has_zhigh
            near += at(c_ref, row - 1) if y > 0 else at(ylow_ref, s) * has_ylow
            near += at(c_ref, row + 1) if y < 7 else at(yhigh_ref, s) * has_yhigh
            near += jnp.where(lane == 0, 0.0, pltpu.roll(c, 1, 1)) + jnp.where(lane == 127, 0.0, pltpu.roll(c, 127, 1))
            next_ref[:, row * 128 : row * 128 + 128] = c - (STEP * SMOOTH) * (6.0 * c - near)


def gradient_step(harm_t, got, next_ref, chunk):
    both = jnp.concatenate([got[:, chunk * 4 + r].reshape(64, 128) for r in range(4)], axis=1)
    cols = pl.ds(chunk * 512, 512)
    new = next_ref[:, cols] - STEP * dot(harm_t, both)
    next_ref[:, cols] = new
    return new


def middle_kernel(
    back_ref, c_ref, harm_ref, harm_t_ref, zlow_ref, zhigh_ref, ylow_ref, yhigh_ref,
    next_ref, field_ref, got, out, send_sem, recv_sem,
):
    angle, x, z, half = position()
    slab = (x * 8 + z) * 2 + half
    rotation = angle * 2 + half
    partners = column_partners(angle, x, z, half)
    greet([target for _, _, _, target in partners])
    copies = send_back(back_ref, got, rotation, partners, send_sem, recv_sem)
    got[rotation] = back_ref[pl.ds(pl.multiple_of(angle * 16, 16), 16)]
    smooth(angle, slab, c_ref, zlow_ref, zhigh_ref, ylow_ref, yhigh_ref, next_ref)
    for copy in copies:
        copy.wait_recv()
    for chunk in range(4):
        new = gradient_step(harm_t_ref[...], got, next_ref, chunk)
        fields = dot(harm_ref[...], new)
        for r in range(4):
            out[:, chunk * 4 + r] = fields[:, r * 128 : r * 128 + 128].reshape(8, 8, 128)
    later = []
    for k, ta, th, target in partners:
        dst = field_ref.at[pl.ds(pl.multiple_of((k % 2) * 64 + angle * 16, 16), 16)]
        later.append(send(out.at[ta * 2 + th], dst, send_sem.at[6 + k], recv_sem.at[6 + k], target))
    field_ref[pl.ds(pl.multiple_of(angle * 16, 16), 16)] = out[rotation]
    for copy in later:
        copy.wait_recv()
    for copy in copies + later:
        copy.wait_send()


def middle(back, c_own, harm_all, harm_t, halos):
    return pl.pallas_call(
        middle_kernel,
        out_shape=(jax.ShapeDtypeStruct((48, 2048), f32), jax.ShapeDtypeStruct((128, 8, 128), f32)),
        in_specs=[VM] * 8,
        out_specs=(VM, VM),
        scratch_shapes=[
            pltpu.VMEM((8, 16, 8, 128), f32),
            pltpu.VMEM((8, 16, 8, 128), f32),
            pltpu.SemaphoreType.DMA((14,)),
            pltpu.SemaphoreType.DMA((14,)),
        ],
        compiler_params=pltpu.CompilerParams(collective_id=2, has_side_effects=True, vmem_limit_bytes=LIMIT),
        name="middle",
    )(back, c_own, harm_all, harm_t, *halos)


def end_kernel(
    back_ref, c_ref, harm_t_ref, zlow_ref, zhigh_ref, ylow_ref, yhigh_ref, own_ref,
    all_ref, mis_ref, next_ref, got, send_sem, recv_sem,
):
    angle, x, z, half = position()
    slab = (x * 8 + z) * 2 + half
    rotation = angle * 2 + half
    other = 1 - half
    partners = column_partners(angle, x, z, half)
    greet([target for _, _, _, target in partners])
    copies = send_back(back_ref, got, rotation, partners, send_sem, recv_sem)
    last = send(own_ref.at[pl.ds(other * 2, 2)], mis_ref.at[half], send_sem.at[7], recv_sem.at[7], device(angle, x, z, other))
    got[rotation] = back_ref[pl.ds(pl.multiple_of(angle * 16, 16), 16)]
    mis_ref[half] = own_ref[pl.ds(half * 2, 2)]
    smooth(angle, slab, c_ref, zlow_ref, zhigh_ref, ylow_ref, yhigh_ref, next_ref)
    for copy in copies:
        copy.wait_recv()
    for chunk in range(4):
        gradient_step(harm_t_ref[...], got, next_ref, chunk)
    later = []
    for k in range(1, 4):
        target = device(lax.rem(angle + k, 4), x, z, half)
        later.append(send(next_ref, all_ref.at[angle], send_sem.at[7 + k], recv_sem.at[7 + k], target))
    all_ref[angle] = next_ref[...]
    for copy in later + [last]:
        copy.wait_recv()
    for copy in copies + later + [last]:
        copy.wait_send()


def end(back, c_own, harm_t, halos, own):
    return pl.pallas_call(
        end_kernel,
        out_shape=(jax.ShapeDtypeStruct((4, 48, 2048), f32), jax.ShapeDtypeStruct((2, 2, 8, 128), f32)),
        in_specs=[VM] * 8,
        out_specs=(VM, VM),
        scratch_shapes=[
            pltpu.VMEM((48, 2048), f32),
            pltpu.VMEM((8, 16, 8, 128), f32),
            pltpu.SemaphoreType.DMA((11,)),
            pltpu.SemaphoreType.DMA((11,)),
        ],
        compiler_params=pltpu.CompilerParams(collective_id=3, has_side_effects=True, vmem_limit_bytes=LIMIT),
        name="end",
    )(back, c_own, harm_t, *halos, own)


def per_device(coefficients, harmonics, stretch, measured, tile_pixel, tile_voxel, tile_shift, tile_count):
    angle = lax.axis_index("angle")
    half = lax.rem(lax.axis_index("slab"), 2)
    tiles = tile_pixel.shape[1]
    c_all = coefficients.reshape(45, 2, 4, 8, 128).transpose(2, 0, 1, 3, 4).reshape(4, 45, 2048)
    c_all = jnp.pad(c_all, ((0, 0), (0, 3), (0, 0)))
    harm = jnp.pad(harmonics.reshape(16, 45), ((0, 0), (0, 83)))
    valid = jnp.arange(tiles)[None, :] < tile_count
    row = lax.rem(lax.div(tile_voxel, 8), 4) * 16 + lax.div(tile_voxel, 32) * 8 + lax.rem(tile_voxel, 8)
    pack = jnp.concatenate(
        [tile_pixel.astype(f32), row.astype(f32), jnp.where(valid, tile_shift, FAR), jnp.zeros((2, tiles), f32)], axis=0
    )
    pack = jnp.pad(pack, ((0, 0), (0, 256 - tiles)))
    field, harm_got, pack_got, meas_got = begin(c_all, harm, pack, measured.reshape(16, 256))

    mine = lax.dynamic_index_in_dim(pack.reshape(4, 2, 256), half, 1, keepdims=False)[:, :tiles]
    theirs = lax.dynamic_index_in_dim(pack_got.reshape(4, 2, 256), half, 1, keepdims=False)[:, :tiles]
    theirs = theirs + jnp.array([[0.0], [64.0], [0.0], [0.0]], f32)
    slots_f = jnp.concatenate([mine, theirs], axis=1)
    slots = slots_f[:2].astype(jnp.int32)
    shifts = jnp.broadcast_to(slots_f[2][:, None], (2 * tiles, 128)).reshape(2 * tiles // 8, 8, 128)
    a = lax.dynamic_index_in_dim(stretch, half, 0, keepdims=False)
    stretch2 = jnp.stack([a, 1.0 / a])
    meas_mine = lax.dynamic_index_in_dim(measured, half, 0, keepdims=False)
    meas_theirs = lax.dynamic_index_in_dim(meas_got.reshape(2, 8, 256), half, 0, keepdims=False)
    pair = jnp.where(half == 0, jnp.stack([meas_mine, meas_theirs]), jnp.stack([meas_theirs, meas_mine]))
    meas = pair.reshape(2, 8, 2, 128).transpose(0, 2, 1, 3).reshape(4, 8, 128)
    harm_all = harm_got.reshape(64, 128)[:, :48]
    harm_t = harm_all.T
    c_own = lax.dynamic_index_in_dim(c_all, angle, 0, keepdims=False)

    for iteration in range(2):
        proj = rays(project_kernel, 4, "project", stretch2, slots, shifts, field)
        mis, own, *halos = reduce(proj.reshape(4, 8, 4, 8, 128), meas, c_own)
        back = rays(back_kernel, 2, "back", stretch2, slots, shifts, mis.reshape(128, 8, 128))
        if iteration == 0:
            c_own, field = middle(back, c_own, harm_all, harm_t, halos)
        else:
            c_new, mis_new = end(back, c_own, harm_t, halos, own)
    updated = c_new[:, :45].reshape(4, 45, 2, 8, 128).transpose(1, 2, 0, 3, 4).reshape(45, 2, 32, 128)
    misfit = mis_new.transpose(0, 2, 1, 3).reshape(2, 8, 256)
    return updated, misfit


def solution(mesh):
    in_specs = (
        P(None, "slab", None, None),
        P("angle", None, None),
        P("angle"),
        P("angle", None, "slab"),
        P("angle", "slab"),
        P("angle", "slab"),
        P("angle", "slab"),
        P("angle", "slab"),
    )
    out_specs = (P(None, "slab", None, None), P("angle", None, "slab"))
    return jax.shard_map(per_device, mesh=mesh, in_specs=in_specs, out_specs=out_specs, check_vma=False)
```

time: 1370 us -> 175 us (0.13)
  waiting for transfers between devices: 1050 us -> 0 us
  Pallas kernels: 0 us -> 156 us
  matrix products: 141 us -> 0 us
  other arithmetic: 104 us -> 3.17 us
  local copies, waits for them, and re-layouts: 29.3 us -> 14.1 us
  starting transfers between devices: 14.5 us -> 0 us
    reduce_scatter x2 -> x0, waiting for transfers between devices: 629 us -> none  [per_device(): lax.psum_scatter(partial_sums, 'slab', scatter_dimension=2, tiled=True)]
    all_gather x2 -> x0, waiting for transfers between devices: 295 us -> none  [per_device(): whole_misfit = lax.all_gather(misfit, 'slab', axis=2, tiled=True)]
    pallas_call x0 -> x9, Pallas kernels: none -> 156 us  [the longest x2 58.2 us: reduce(): pl.pallas_call(reduce_kernel, out_shape=(jax.ShapeDtypeStruct((4, 8, 4, 8...]
    dot_general x38 -> x0, matrix products: 141 us -> none  [the longest x16 81.7 us: back_accumulate(): jnp.einsum('stp,tvp->tsv', picked, weights, precision=lax.Precision.HIGHEST)]
    ppermute x4 -> x0, waiting for transfers between devices: 81.2 us -> none  [the longest x2 55.2 us: padded_2(): lax.ppermute(lax.slice_in_dim(block, block.shape[dim] - width, None, axis...]
    scatter-add x32 -> x0, other arithmetic: 70.3 us -> none  [the longest x16 35.2 us: back_accumulate(): return (total.at[block_voxels].add(contrib), None)]
    psum x2 -> x0, waiting for transfers between devices: 47 us -> none  [per_device(): gradient = lax.psum(local_terms, 'angle')]
    gather x32 -> x0, local copies, waits for them, and re-layouts: 19.5 us -> none  [the longest x16 9.73 us: project_accumulate(): picked = seg_field[:, block_voxels, :]]
  transfers between devices with their start and end apart: 10 -> 0, of which waited for: 10 -> 0; matrix products, arithmetic and copies ran while one was open for 0% -> 0% of each run, Pallas kernels for 0% -> 0%
where the time goes in v1:
time: 175 us
  Pallas kernels  156 us (89%)
  local copies, waits for them, and re-layouts  14.1 us (8%)
  other arithmetic  3.17 us (2%)
    pallas_call x2, Pallas kernels, reduce(): pl.pallas_call(reduce_kernel, out_shape=(jax.ShapeDtypeStruct((4, 8, 4, 8...  58.2 us
    pallas_call x4, Pallas kernels, rays(): pl.pallas_call(body, out_shape=jax.ShapeDtypeStruct((128, 8, 128), f32),...  31.6 us
    pallas_call x1, Pallas kernels, end(): pl.pallas_call(end_kernel, out_shape=(jax.ShapeDtypeStruct((4, 48, 2048),...  31.5 us
    pallas_call x1, Pallas kernels, middle(): pl.pallas_call(middle_kernel, out_shape=(jax.ShapeDtypeStruct((48, 2048),...  22.3 us
    pallas_call x1, Pallas kernels, begin(): pl.pallas_call(begin_kernel, out_shape=(jax.ShapeDtypeStruct((128, 8, 128...  12.7 us
    reshape x2, local copies, waits for them, and re-layouts, per_device(): coefficients.reshape(45, 2, 4, 8, 128).transpose(2, 0, 1, 3, 4)  4.94 us
    reshape x2, local copies, waits for them, and re-layouts, per_device(): c_new[:, :45].reshape(4, 45, 2, 8, 128).transpose(1, 2, 0, 3, 4)  4.07 us

profile of v1, /device:TPU:1, one launch (start us, length us, event | category | flops | bytes accessed | tf_op | source)
XLA Modules:
  0.0 175.1 jit_solution(7056323445043343730)
XLA Ops:
  0.6 0.0 copy-start
  0.7 1.4 dynamic_slice.22
  2.7 0.7 pad_maximum_fusion.2.stretch_ref
  3.4 0.1 pad.26.clone
  3.5 0.7 convert_element_type.15
  4.2 0.7 fusion.6
  4.9 0.8 compare_select_fusion.2
  5.6 0.1 maximum_maximum_fusion
  5.7 0.7 pad.14.harm_ref
  6.4 1.2 copy_bitcast_fusion.1
  7.7 2.7 %reshape.65 = f32[4,45,2048]{2,0,1:T(4,128)} reshape(f32[4,45,2,8,128]{4,3,2,0,1:T(8,128)} %copy_bitcast_fusion.1) | data formatting | bytes 2949120 | tf_op jit(solution)/shard_map/reshape | solution.py:422
  10.4 2.2 %copy.26 = f32[4,45,2048]{2,1,0:T(8,128)S(1)} copy(f32[4,45,2048]{2,0,1:T(4,128)} %reshape.65) | data formatting | bytes 2949120 | tf_op jit(solution)/shard_map/reshape | solution.py:422
  12.7 0.2 pad.13.c_ref
  12.8 0.5 copy-done.1
  13.4 12.7 %begin.1 = (f32[128,8,128]{2,1,0:T(8,128)S(1)}, f32[4,16,128]{2,1,0:T(8,128)S(1)}, f32[8,256]{1,0:T(8,128)S(1)}, f32[16,256]{1,0:T(8,128)S(1)}) custom-call(f32[4,48,2048]{2,1,0:T(8,128)S(1)} %pad.13.c_ref, f32[16,128]{1,0:T(8,128)S(1)} %pad.14.harm_ref, f32[8,256]{1,0:T(8,128)S(1)} %pad.12.pack_ref, f32[16,256]{1,0:T(8,128)S(1)} %bitcast.51), custom_call_target="tpu_custom_call" | custom-call | tf_op jit(solution)/shard_map/begin/pallas_call | solution.py:78
  26.2 0.1 slice_add_fusion
  26.3 0.1 fusion.7
  26.4 0.1 fusion.1.slot_ref
  26.4 0.1 broadcast_in_dim.17
  26.5 0.1 copy.36
  26.6 0.1 broadcast_in_dim.18.shift_ref
  26.7 9.2 %project.2 = f32[128,8,128]{2,1,0:T(8,128)S(1)} custom-call(f32[2]{0:T(128)S(1)} %pad_maximum_fusion.2.stretch_ref, s32[2,384]{1,0:T(2,128)S(1)} %fusion.1.slot_ref, f32[48,8,128]{2,1,0:T(8,128)S(1)} %broadcast_in_dim.18.shift_ref, f32[128,8,128]{2,1,0:T(8,128)S(1)} %get-tuple-element.22.field_ref), custom_call_target="tpu_custom_call" | custom-call | tf_op jit(solution)/shard_map/project/pallas_call | solution.py:169
  35.9 32.8 %reduce.4 = (f32[4,8,4,8,128]{4,3,2,1,0:T(8,128)S(1)}, f32[4,8,128]{2,1,0:T(8,128)}, f32[48,1024]{1,0:T(8,128)S(1)}, f32[48,1024]{1,0:T(8,128)S(1)}, f32[48,256]{1,0:T(8,128)S(1)}, /*index=5*/f32[48,256]{1,0:T(8,128)S(1)}) custom-call(f32[4,8,4,8,128]{4,3,2,1,0:T(8,128)S(1)} %bitcast.41, f32[4,8,128]{2,1,0:T(8,128)S(1)} %bitcast.47, ...), custom_call_target="tpu_custom_call" | custom-call | tf_op jit(solution)/shard_map/reduce/pallas_call | solution.py:252
  68.7 6.6 %back.2.back_ref = f32[128,8,128]{2,1,0:T(8,128)S(1)} custom-call(f32[2]{0:T(128)S(1)} %pad_maximum_fusion.2.stretch_ref, s32[2,384]{1,0:T(2,128)S(1)} %fusion.1.slot_ref, f32[48,8,128]{2,1,0:T(8,128)S(1)} %broadcast_in_dim.18.shift_ref, f32[128,8,128]{2,1,0:T(8,128)S(1)} %bitcast.44), custom_call_target="tpu_custom_call" | custom-call | tf_op jit(solution)/shard_map/back/pallas_call | solution.py:169
  75.3 22.3 %middle.1 = (f32[48,2048]{1,0:T(8,128)S(1)}, f32[128,8,128]{2,1,0:T(8,128)S(1)}) custom-call(f32[128,8,128]{2,1,0:T(8,128)S(1)} %back.2.back_ref, f32[48,2048]{1,0:T(8,128)S(1)} %dynamic-slice_bitcast_fusion.c_ref, f32[64,48]{1,0:T(8,128)S(1)} %bitcast.50, f32[48,64]{1,0:T(8,128)S(1)} %bitcast.45, f32[48,1024]{1,0:T(8,128)S(1)} %get-tuple-element.26.zlow_ref, ...), custom_call_target="tpu_custom_call" | custom-call | tf_op jit(solution)/shard_map/middle/pallas_call | solution.py:355
  97.7 9.2 %project.3 = f32[128,8,128]{2,1,0:T(8,128)S(1)} custom-call(f32[2]{0:T(128)S(1)} %pad_maximum_fusion.2.stretch_ref, s32[2,384]{1,0:T(2,128)S(1)} %fusion.1.slot_ref, f32[48,8,128]{2,1,0:T(8,128)S(1)} %broadcast_in_dim.18.shift_ref, f32[128,8,128]{2,1,0:T(8,128)S(1)} %get-tuple-element.30.field_ref), custom_call_target="tpu_custom_call" | custom-call | tf_op jit(solution)/shard_map/project/pallas_call | solution.py:169
  106.8 25.4 %reduce.5 = (f32[4,8,4,8,128]{4,3,2,1,0:T(8,128)S(1)}, f32[4,8,128]{2,1,0:T(8,128)S(1)}, f32[48,1024]{1,0:T(8,128)S(1)}, f32[48,1024]{1,0:T(8,128)S(1)}, f32[48,256]{1,0:T(8,128)S(1)}, /*index=5*/f32[48,256]{1,0:T(8,128)S(1)}) custom-call(f32[4,8,4,8,128]{4,3,2,1,0:T(8,128)S(1)} %bitcast.40, f32[4,8,128]{2,1,0:T(8,128)S(1)} %bitcast.48, ...), custom_call_target="tpu_custom_call" | custom-call | tf_op jit(solution)/shard_map/reduce/pallas_call | solution.py:252
  132.3 6.6 %back.3.back_ref = f32[128,8,128]{2,1,0:T(8,128)S(1)} custom-call(f32[2]{0:T(128)S(1)} %pad_maximum_fusion.2.stretch_ref, s32[2,384]{1,0:T(2,128)S(1)} %fusion.1.slot_ref, f32[48,8,128]{2,1,0:T(8,128)S(1)} %broadcast_in_dim.18.shift_ref, f32[128,8,128]{2,1,0:T(8,128)S(1)} %bitcast.43), custom_call_target="tpu_custom_call" | custom-call | tf_op jit(solution)/shard_map/back/pallas_call | solution.py:169
  138.9 31.5 %end.1 = (f32[4,48,2048]{2,1,0:T(8,128)S(1)}, f32[2,2,8,128]{3,2,1,0:T(8,128)S(1)}) custom-call(f32[128,8,128]{2,1,0:T(8,128)S(1)} %back.3.back_ref, f32[48,2048]{1,0:T(8,128)S(1)} %get-tuple-element.31.c_ref, f32[48,64]{1,0:T(8,128)S(1)} %bitcast.46, f32[48,1024]{1,0:T(8,128)S(1)} %get-tuple-element.33.zlow_ref, ...), custom_call_target="tpu_custom_call" | custom-call | tf_op jit(solution)/shard_map/end/pallas_call | solution.py:402
  170.4 1.4 reshape.79
  171.8 2.7 %copy_bitcast_fusion = f32[45,2,32,128]{3,2,1,0:T(8,128)} fusion(f32[4,45,2,8,128]{4,3,2,1,0:T(8,128)} %reshape.79), kind=kLoop, calls=%fused_computation | loop fusion | bytes 2949120 | tf_op jit(solution)/shard_map/reshape | solution.py:457
  174.5 0.6 copy.44
  (16 shorter events, 0.1 us)
Async XLA Ops:
  0.6 5.8 %copy-start = (f32[45,2,32,128]{3,2,1,0:T(8,128)S(1)}, f32[45,2,32,128]{3,2,1,0:T(8,128)}, u32[]{:S(2)}) copy-start(f32[45,2,32,128]{3,2,1,0:T(8,128)} %param.9) | copy-start | bytes 4423684
  12.7 0.7 copy-start.1
  13.4 12.8 %copy-start.2 = (f32[4]{0:T(128)S(1)}, f32[4]{0:T(128)}, u32[]{:S(2)}) copy-start(f32[4]{0:T(128)} %constant.79) | copy-start | bytes 52

commit v2 on v1

--- a/solution.py
+++ b/solution.py
@@ -15,6 +15,9 @@
 VM = pl.BlockSpec(memory_space=pltpu.VMEM)
 SM = pl.BlockSpec(memory_space=pltpu.SMEM)
 LIMIT = 48 * 2**20
+DN = lax.GatherDimensionNumbers(
+    offset_dims=(), collapsed_slice_dims=(1,), start_index_map=(1,), operand_batching_dims=(0,), start_indices_batching_dims=(0,)
+)
 
 
 def position():
@@ -335,6 +338,18 @@
     smooth(angle, slab, c_ref, zlow_ref, zhigh_ref, ylow_ref, yhigh_ref, next_ref)
     for copy in copies:
         copy.wait_recv()
+    probe = c_ref[0:8, 0:128]
+    i0 = jnp.floor(probe).astype(jnp.int32) & 127
+    picked = lax.gather(probe, i0[..., None], DN, slice_sizes=(1, 1), mode=lax.GatherScatterMode.PROMISE_IN_BOUNDS)
+    ids = lax.broadcasted_iota(jnp.int32, (64, 64), 1)
+    hot = jnp.where(ids == i0[0:1, :64], 1.0, 0.0).astype(jnp.bfloat16)
+    hit = jnp.dot(hot, got[0, 0:8, :, :].reshape(64, 128).astype(jnp.bfloat16), preferred_element_type=f32)
+
+    def step(i, carry):
+        next_ref[pl.ds(pl.multiple_of(i * 8, 8), 8), :128] += jnp.minimum(jnp.abs(picked + hit[:8]), 0.0)
+        return carry
+
+    lax.fori_loop(0, 6, step, 0)
     for chunk in range(4):
         new = gradient_step(harm_t_ref[...], got, next_ref, chunk)
         fields = dot(harm_ref[...], new)

time: 175 us -> 176 us (level)
  no operation moved by 1% of the time
where the time goes in v2:
time: 176 us; the launch traced here: 175 us
  Pallas kernels  157 us (89%)
  local copies, waits for them, and re-layouts  14.1 us (8%)
  other arithmetic  3.17 us (2%)
    pallas_call x2, Pallas kernels, reduce(): pl.pallas_call(reduce_kernel, out_shape=(jax.ShapeDtypeStruct((4, 8, 4, 8...  58.3 us
    pallas_call x4, Pallas kernels, rays(): pl.pallas_call(body, out_shape=jax.ShapeDtypeStruct((128, 8, 128), f32),...  31.6 us
    pallas_call x1, Pallas kernels, end(): pl.pallas_call(end_kernel, out_shape=(jax.ShapeDtypeStruct((4, 48, 2048),...  31.5 us
    pallas_call x1, Pallas kernels, middle(): pl.pallas_call(middle_kernel, out_shape=(jax.ShapeDtypeStruct((48, 2048),...  22.5 us
    pallas_call x1, Pallas kernels, begin(): pl.pallas_call(begin_kernel, out_shape=(jax.ShapeDtypeStruct((128, 8, 128...  12.7 us
    reshape x2, local copies, waits for them, and re-layouts, per_device(): coefficients.reshape(45, 2, 4, 8, 128).transpose(2, 0, 1, 3, 4)  4.94 us
    reshape x2, local copies, waits for them, and re-layouts, per_device(): c_new[:, :45].reshape(4, 45, 2, 8, 128).transpose(1, 2, 0, 3, 4)  4.07 us

profile of v2, /device:TPU:1, one launch (start us, length us, event | category | flops | bytes accessed | tf_op | source)
XLA Modules:
  0.0 175.3 jit_solution(6606890844994924562)
XLA Ops:
  0.6 0.0 copy-start
  0.7 1.4 dynamic_slice.22
  2.7 0.7 pad_maximum_fusion.2.stretch_ref
  3.4 0.1 pad.26.clone
  3.5 0.7 convert_element_type.15
  4.2 0.7 fusion.6
  4.9 0.8 compare_select_fusion.2
  5.6 0.1 maximum_maximum_fusion
  5.7 0.7 pad.14.harm_ref
  6.4 1.2 copy_bitcast_fusion.1
  7.7 2.7 %reshape.65 = f32[4,45,2048]{2,0,1:T(4,128)} reshape(f32[4,45,2,8,128]{4,3,2,0,1:T(8,128)} %copy_bitcast_fusion.1) | data formatting | bytes 2949120 | tf_op jit(solution)/shard_map/reshape | solution.py:437
  10.4 2.2 %copy.26 = f32[4,45,2048]{2,1,0:T(8,128)S(1)} copy(f32[4,45,2048]{2,0,1:T(4,128)} %reshape.65) | data formatting | bytes 2949120 | tf_op jit(solution)/shard_map/reshape | solution.py:437
  12.7 0.2 pad.13.c_ref
  12.8 0.5 copy-done.1
  13.4 12.7 %begin.1 = (f32[128,8,128]{2,1,0:T(8,128)S(1)}, f32[4,16,128]{2,1,0:T(8,128)S(1)}, f32[8,256]{1,0:T(8,128)S(1)}, f32[16,256]{1,0:T(8,128)S(1)}) custom-call(f32[4,48,2048]{2,1,0:T(8,128)S(1)} %pad.13.c_ref, f32[16,128]{1,0:T(8,128)S(1)} %pad.14.harm_ref, f32[8,256]{1,0:T(8,128)S(1)} %pad.12.pack_ref, f32[16,256]{1,0:T(8,128)S(1)} %bitcast.51), custom_call_target="tpu_custom_call" | custom-call | tf_op jit(solution)/shard_map/begin/pallas_call | solution.py:81
  26.2 0.1 slice_add_fusion
  26.3 0.1 fusion.7
  26.4 0.1 fusion.1.slot_ref
  26.4 0.1 broadcast_in_dim.17
  26.5 0.1 copy.36
  26.6 0.1 broadcast_in_dim.18.shift_ref
  26.7 9.2 %project.2 = f32[128,8,128]{2,1,0:T(8,128)S(1)} custom-call(f32[2]{0:T(128)S(1)} %pad_maximum_fusion.2.stretch_ref, s32[2,384]{1,0:T(2,128)S(1)} %fusion.1.slot_ref, f32[48,8,128]{2,1,0:T(8,128)S(1)} %broadcast_in_dim.18.shift_ref, f32[128,8,128]{2,1,0:T(8,128)S(1)} %get-tuple-element.22.field_ref), custom_call_target="tpu_custom_call" | custom-call | tf_op jit(solution)/shard_map/project/pallas_call | solution.py:172
  35.9 32.8 %reduce.4 = (f32[4,8,4,8,128]{4,3,2,1,0:T(8,128)S(1)}, f32[4,8,128]{2,1,0:T(8,128)}, f32[48,1024]{1,0:T(8,128)S(1)}, f32[48,1024]{1,0:T(8,128)S(1)}, f32[48,256]{1,0:T(8,128)S(1)}, /*index=5*/f32[48,256]{1,0:T(8,128)S(1)}) custom-call(f32[4,8,4,8,128]{4,3,2,1,0:T(8,128)S(1)} %bitcast.41, f32[4,8,128]{2,1,0:T(8,128)S(1)} %bitcast.47, ...), custom_call_target="tpu_custom_call" | custom-call | tf_op jit(solution)/shard_map/reduce/pallas_call | solution.py:255
  68.7 6.6 %back.2.back_ref = f32[128,8,128]{2,1,0:T(8,128)S(1)} custom-call(f32[2]{0:T(128)S(1)} %pad_maximum_fusion.2.stretch_ref, s32[2,384]{1,0:T(2,128)S(1)} %fusion.1.slot_ref, f32[48,8,128]{2,1,0:T(8,128)S(1)} %broadcast_in_dim.18.shift_ref, f32[128,8,128]{2,1,0:T(8,128)S(1)} %bitcast.44), custom_call_target="tpu_custom_call" | custom-call | tf_op jit(solution)/shard_map/back/pallas_call | solution.py:172
  75.3 22.5 %middle.1 = (f32[48,2048]{1,0:T(8,128)S(1)}, f32[128,8,128]{2,1,0:T(8,128)S(1)}) custom-call(f32[128,8,128]{2,1,0:T(8,128)S(1)} %back.2.back_ref, f32[48,2048]{1,0:T(8,128)S(1)} %dynamic-slice_bitcast_fusion.c_ref, f32[64,48]{1,0:T(8,128)S(1)} %bitcast.50, f32[48,64]{1,0:T(8,128)S(1)} %bitcast.45, f32[48,1024]{1,0:T(8,128)S(1)} %get-tuple-element.26.zlow_ref, ...), custom_call_target="tpu_custom_call" | custom-call | tf_op jit(solution)/shard_map/middle/pallas_call | solution.py:370
  97.8 9.2 %project.3 = f32[128,8,128]{2,1,0:T(8,128)S(1)} custom-call(f32[2]{0:T(128)S(1)} %pad_maximum_fusion.2.stretch_ref, s32[2,384]{1,0:T(2,128)S(1)} %fusion.1.slot_ref, f32[48,8,128]{2,1,0:T(8,128)S(1)} %broadcast_in_dim.18.shift_ref, f32[128,8,128]{2,1,0:T(8,128)S(1)} %get-tuple-element.30.field_ref), custom_call_target="tpu_custom_call" | custom-call | tf_op jit(solution)/shard_map/project/pallas_call | solution.py:172
  107.0 25.5 %reduce.5 = (f32[4,8,4,8,128]{4,3,2,1,0:T(8,128)S(1)}, f32[4,8,128]{2,1,0:T(8,128)S(1)}, f32[48,1024]{1,0:T(8,128)S(1)}, f32[48,1024]{1,0:T(8,128)S(1)}, f32[48,256]{1,0:T(8,128)S(1)}, /*index=5*/f32[48,256]{1,0:T(8,128)S(1)}) custom-call(f32[4,8,4,8,128]{4,3,2,1,0:T(8,128)S(1)} %bitcast.40, f32[4,8,128]{2,1,0:T(8,128)S(1)} %bitcast.48, ...), custom_call_target="tpu_custom_call" | custom-call | tf_op jit(solution)/shard_map/reduce/pallas_call | solution.py:255
  132.5 6.6 %back.3.back_ref = f32[128,8,128]{2,1,0:T(8,128)S(1)} custom-call(f32[2]{0:T(128)S(1)} %pad_maximum_fusion.2.stretch_ref, s32[2,384]{1,0:T(2,128)S(1)} %fusion.1.slot_ref, f32[48,8,128]{2,1,0:T(8,128)S(1)} %broadcast_in_dim.18.shift_ref, f32[128,8,128]{2,1,0:T(8,128)S(1)} %bitcast.43), custom_call_target="tpu_custom_call" | custom-call | tf_op jit(solution)/shard_map/back/pallas_call | solution.py:172
  139.1 31.5 %end.1 = (f32[4,48,2048]{2,1,0:T(8,128)S(1)}, f32[2,2,8,128]{3,2,1,0:T(8,128)S(1)}) custom-call(f32[128,8,128]{2,1,0:T(8,128)S(1)} %back.3.back_ref, f32[48,2048]{1,0:T(8,128)S(1)} %get-tuple-element.31.c_ref, f32[48,64]{1,0:T(8,128)S(1)} %bitcast.46, f32[48,1024]{1,0:T(8,128)S(1)} %get-tuple-element.33.zlow_ref, ...), custom_call_target="tpu_custom_call" | custom-call | tf_op jit(solution)/shard_map/end/pallas_call | solution.py:417
  170.7 1.4 reshape.79
  172.1 2.7 %copy_bitcast_fusion = f32[45,2,32,128]{3,2,1,0:T(8,128)} fusion(f32[4,45,2,8,128]{4,3,2,1,0:T(8,128)} %reshape.79), kind=kLoop, calls=%fused_computation | loop fusion | bytes 2949120 | tf_op jit(solution)/shard_map/reshape | solution.py:472
  174.7 0.6 copy.44
  (16 shorter events, 0.1 us)
Async XLA Ops:
  0.6 5.8 %copy-start = (f32[45,2,32,128]{3,2,1,0:T(8,128)S(1)}, f32[45,2,32,128]{3,2,1,0:T(8,128)}, u32[]{:S(2)}) copy-start(f32[45,2,32,128]{3,2,1,0:T(8,128)} %param.9) | copy-start | bytes 4423684
  12.7 0.7 copy-start.1
  13.4 12.8 %copy-start.2 = (f32[4]{0:T(128)S(1)}, f32[4]{0:T(128)}, u32[]{:S(2)}) copy-start(f32[4]{0:T(128)} %constant.79) | copy-start | bytes 52

commit v3 on v0

v3 whole, which is shorter than its diff:
```python
import jax
import jax.numpy as jnp
from jax import lax
from jax.experimental import pallas as pl
from jax.experimental.pallas import tpu as pltpu
from jax.sharding import PartitionSpec as P

f32 = jnp.float32
bf16 = jnp.bfloat16
MESH = pl.DeviceIdType.MESH
STEP = 0.003
SMOOTH = 6.0
FAR = 1.0e6
TS = 192
CHUNK = 48
TAKE = lax.GatherDimensionNumbers(
    offset_dims=(), collapsed_slice_dims=(1,), start_index_map=(1,), operand_batching_dims=(0,), start_indices_batching_dims=(0,)
)

VM = pl.BlockSpec(memory_space=pltpu.VMEM)
SM = pl.BlockSpec(memory_space=pltpu.SMEM)
LIMIT = 48 * 2**20


def position():
    angle = lax.axis_index("angle")
    slab = lax.axis_index("slab")
    return angle, lax.div(slab, 16), lax.rem(lax.div(slab, 2), 8), lax.rem(slab, 2)


def device(angle, x, z, half):
    return (angle, (x * 8 + z) * 2 + half)


def signal(partners):
    barrier = pltpu.get_barrier_semaphore()
    for partner in partners:
        pl.semaphore_signal(barrier, inc=1, device_id=partner, device_id_type=MESH)


def await_signals(partners):
    pl.semaphore_wait(pltpu.get_barrier_semaphore(), len(partners))


def send(src, dst, send_sem, recv_sem, target):
    pltpu.make_async_remote_copy(
        src_ref=src, dst_ref=dst, send_sem=send_sem, recv_sem=recv_sem, device_id=target, device_id_type=MESH
    ).start()


def drain(like, sem):
    pltpu.make_async_copy(like, like, sem).wait()


def dot(a, b):
    return jnp.dot(a, b, preferred_element_type=f32, precision=lax.Precision.HIGHEST)


def hot(a, b):
    return jnp.dot(a, b, preferred_element_type=f32)


def parts(value, count):
    found = []
    for _ in range(count - 1):
        part = value.astype(bf16)
        found.append(part)
        value = value - part.astype(f32)
    return found + [value.astype(bf16)]


def take(values, lanes):
    return lax.gather(values, lanes[..., None], TAKE, slice_sizes=(1, 1), mode=lax.GatherScatterMode.PROMISE_IN_BOUNDS)


def begin_kernel(
    harm_s, c_ref, harm_ref, pix_ref, vox_ref, shift_ref, count_ref, meas_ref,
    field_ref, harm_all_ref, packs_ref, own_ref, blocks, pack, send_sem, recv_sem,
):
    angle, x, z, half = position()
    slab = x * 2 + half
    peers = [device(angle, lax.rem(x + k // 2, 4), z, lax.rem(half + k % 2, 2)) for k in range(1, 8)]
    angles = [device(lax.rem(angle + k, 4), x, z, half) for k in range(1, 4)]
    signal(peers + angles)

    valid = lax.broadcasted_iota(jnp.int32, (2, TS), 1) < count_ref[...]
    pack[...] = jnp.zeros_like(pack)
    pack[0:2, :TS] = pix_ref[...].astype(f32)
    pack[2:4, :TS] = vox_ref[...].astype(f32)
    pack[4:6, :TS] = jnp.where(valid, shift_ref[...], FAR)
    pack[8:16] = meas_ref[0]
    pack[16:24] = meas_ref[1]
    packs_ref[slab] = pack[...]
    harm_all_ref[angle] = jnp.zeros((16, 128), f32)
    harm_all_ref[angle, 0:8, 0:45] = harm_ref[0]
    harm_all_ref[angle, 8:16, 0:45] = harm_ref[1]
    quarter = pl.ds(pl.multiple_of(angle * 8, 8), 8)
    own_ref[:45, :, 0:128] = c_ref[:, 0, quarter, :]
    own_ref[:45, :, 128:256] = c_ref[:, 1, quarter, :]
    own_ref[45:] = jnp.zeros((3, 8, 256), f32)
    await_signals(peers + angles)
    for target in peers:
        send(pack, packs_ref.at[slab], send_sem.at[0], recv_sem.at[0], target)
    for target in angles:
        send(harm_all_ref.at[angle], harm_all_ref.at[angle], send_sem.at[1], recv_sem.at[1], target)

    def fields(which, segments, dest):
        for s in range(2):
            channel = which * 8 + segments * 2 + s
            for zz in range(2):
                sums = [None] * 4
                for k in range(45):
                    h = harm_s[channel, k]
                    for y in range(4):
                        term = c_ref[k, zz, y * 8 : y * 8 + 8, :] * h
                        sums[y] = term if k == 0 else sums[y] + term
                for y in range(4):
                    dest[y, s, :, zz * 128 : zz * 128 + 128] = sums[y]

    def block(i, carry):
        xx, hh = lax.rem(x + lax.div(i, 2), 4), lax.rem(half + lax.rem(i, 2), 2)
        fields(hh, xx, blocks.at[i - 1])
        send(blocks.at[i - 1], field_ref.at[slab], send_sem.at[2], recv_sem.at[2], device(angle, xx, z, hh))
        return carry

    lax.fori_loop(1, 8, block, 0)
    fields(half, x, field_ref.at[slab])
    for sems in (recv_sem, send_sem):
        drain(packs_ref.at[pl.ds(0, 7)], sems.at[0])
        drain(harm_all_ref.at[pl.ds(0, 3)], sems.at[1])
        drain(field_ref.at[pl.ds(0, 7)], sems.at[2])


def begin(coefficients, harmonics, tile_pixel, tile_voxel, tile_shift, tile_count, measured):
    return pl.pallas_call(
        begin_kernel,
        out_shape=(
            jax.ShapeDtypeStruct((8, 4, 2, 8, 256), f32),
            jax.ShapeDtypeStruct((4, 16, 128), f32),
            jax.ShapeDtypeStruct((8, 24, 256), f32),
            jax.ShapeDtypeStruct((48, 8, 256), f32),
        ),
        in_specs=[SM] + [VM] * 7,
        out_specs=(VM,) * 4,
        scratch_shapes=[
            pltpu.VMEM((7, 4, 2, 8, 256), f32),
            pltpu.VMEM((24, 256), f32),
            pltpu.SemaphoreType.DMA((3,)),
            pltpu.SemaphoreType.DMA((3,)),
        ],
        compiler_params=pltpu.CompilerParams(collective_id=0, has_side_effects=True, vmem_limit_bytes=LIMIT),
        name="begin",
    )(harmonics.reshape(16, 45), coefficients, harmonics, tile_pixel, tile_voxel, tile_shift, tile_count, measured)


def project_slab(sl, a, inv, shift_ref, pick_ref, field, picked, contrib):
    rows = [
        jnp.concatenate([field[sl, y, s, :, zz * 128 : zz * 128 + 128] for s in range(2)], axis=1)
        for zz in range(2)
        for y in range(4)
    ]
    split = jnp.concatenate(parts(jnp.concatenate(rows, axis=0), 3), axis=0)
    picked[...] = hot(pick_ref[pl.ds(pl.multiple_of(sl * TS, TS), TS), :], split)
    lane = lax.broadcasted_iota(jnp.int32, (CHUNK, 128), 1).astype(f32)
    for c in range(TS // CHUNK):
        at = pl.ds(pl.multiple_of(sl * TS + c * CHUNK, 16), CHUNK)
        u = lane - shift_ref[at, :]
        v0 = jnp.floor((u - 1.0) * inv) + 1.0
        t0 = u - a * v0
        first = v0.astype(jnp.int32)
        taps = (1.0 - t0, 1.0 - jnp.abs(t0 - a), 1.0 + t0 - 2.0 * a, 1.0 + t0 - 3.0 * a)
        lanes, weights = [], []
        for k in range(4):
            v = first + k
            inside = v & 127
            lanes.append(inside)
            weights.append(jnp.where(v == inside, jnp.maximum(taps[k], 0.0), 0.0))
        for s in range(2):
            f = picked[c * CHUNK : (c + 1) * CHUNK, s * 128 : s * 128 + 128]
            terms = [take(f, lanes[k]) * weights[k] for k in range(4)]
            contrib[at, s * 128 : s * 128 + 128] = (terms[0] + terms[1]) + (terms[2] + terms[3])


def back_slab(sl, a, shift_ref, pick_ref, sum_ref, split, picked, contrib, back):
    picked[...] = hot(pick_ref[pl.ds(pl.multiple_of(sl * TS, TS), TS), :], split[...])
    lane = lax.broadcasted_iota(jnp.int32, (CHUNK, 128), 1).astype(f32)
    for c in range(TS // CHUNK):
        at = slice(c * CHUNK, (c + 1) * CHUNK)
        t = shift_ref[pl.ds(pl.multiple_of(sl * TS + c * CHUNK, 16), CHUNK), :] + a * lane
        p0 = jnp.floor(t)
        w1 = t - p0
        w0 = jnp.where(p0 <= 127.0, 1.0 - w1, 0.0)
        w1 = jnp.where(p0 <= 126.0, w1, 0.0)
        first = p0.astype(jnp.int32)
        lane0, lane1 = first & 127, (first + 1) & 127
        for s in range(2):
            m = picked[at, s * 128 : s * 128 + 128]
            contrib[at, s * 128 : s * 128 + 128] = take(m, lane0) * w0 + take(m, lane1) * w1
    high, low = parts(contrib[:TS], 2)
    total = hot(sum_ref[sl], high) + hot(sum_ref[sl], low)
    for y in range(4):
        for s in range(2):
            for zz in range(2):
                row = zz * 32 + y * 8
                back[sl, y, s, :, zz * 128 : zz * 128 + 128] = total[row : row + 8, s * 128 : s * 128 + 128]


def smooth(angle, slab, c_ref, zlow, zhigh, ylow, yhigh, next_ref):
    lane = lax.broadcasted_iota(jnp.int32, (8, 128), 1)
    sub = lax.broadcasted_iota(jnp.int32, (8, 128), 0)
    has_zlow = (slab > 0).astype(f32)
    has_zhigh = (slab < 63).astype(f32)
    has_ylow = (angle > 0).astype(f32)
    has_yhigh = (angle < 3).astype(f32)

    def one(k, carry):
        c = c_ref[k]
        below, above = ylow[pl.ds(k, 1), :] * has_ylow, yhigh[pl.ds(k, 1), :] * has_yhigh
        half = (c[:, :128], c[:, 128:])
        deep = (zlow[k] * has_zlow + half[1], half[0] + zhigh[k] * has_zhigh)
        for zz in range(2):
            v = half[zz]
            at = slice(zz * 128, zz * 128 + 128)
            near = deep[zz]
            near += jnp.where(sub == 0, jnp.broadcast_to(below[:, at], (8, 128)), pltpu.roll(v, 1, 0))
            near += jnp.where(sub == 7, jnp.broadcast_to(above[:, at], (8, 128)), pltpu.roll(v, 7, 0))
            near += jnp.where(lane == 0, 0.0, pltpu.roll(v, 1, 1)) + jnp.where(lane == 127, 0.0, pltpu.roll(v, 127, 1))
            next_ref[k, :, at] = v - (STEP * SMOOTH) * (6.0 * v - near)
        return carry

    lax.fori_loop(0, 48, one, 0, unroll=4)


def main_kernel(
    stretch_ref, shift_ref, pick_v, sum_p, pick_p, sum_v, meas_ref, field0, c0_ref, harm_f, harm_t,
    out_ref, mout_ref,
    field1, c1_ref, next_ref, proj, sums, misfit, picked, contrib, split, back, got, fields, zlow, zhigh, ylow, yhigh, edges,
    send_sem, recv_sem,
):
    angle, x, z, half = position()
    slab = (x * 8 + z) * 2 + half
    mine = x * 2 + half
    block = (angle * 2 + half) * 4 + x
    a = stretch_ref[0]
    inv = stretch_ref[1]
    plane = [
        device(lax.rem(angle + k // 8, 4), lax.rem(x + k // 2, 4), z, lax.rem(half + k % 2, 2)) for k in range(1, 32)
    ]
    line = [device(angle, x, lax.rem(z + k, 8), half) for k in range(1, 8)]
    beyond = (angle, lax.rem(slab + 2 * half + 63, 64))
    partners = plane + line + [beyond]
    above = (angle, lax.rem(slab + 1, 64))
    below = (angle, lax.rem(slab + 63, 64))
    right = (lax.rem(angle + 1, 4), slab)
    left = (lax.rem(angle + 3, 4), slab)
    signal(partners)

    def halos(it, c_ref):
        base = it * 8
        edges[it, 0] = c_ref[:, 7, :]
        edges[it, 1] = c_ref[:, 0, :]
        send(c_ref.at[:, :, pl.ds(128, 128)], zlow.at[it], send_sem.at[base + 4], recv_sem.at[base + 4], above)
        send(c_ref.at[:, :, pl.ds(0, 128)], zhigh.at[it], send_sem.at[base + 5], recv_sem.at[base + 5], below)
        send(edges.at[it, 0], ylow.at[it], send_sem.at[base + 6], recv_sem.at[base + 6], right)
        send(edges.at[it, 1], yhigh.at[it], send_sem.at[base + 7], recv_sem.at[base + 7], left)

    def drain_halos(it, sems):
        base = it * 8
        drain(zlow.at[it], sems.at[base + 4])
        drain(zhigh.at[it], sems.at[base + 5])
        drain(ylow.at[it], sems.at[base + 6])
        drain(yhigh.at[it], sems.at[base + 7])

    for it in range(2):
        base = it * 8
        field = field0 if it == 0 else field1
        c_ref = c0_ref if it == 0 else c1_ref

        def project(sl, carry):
            project_slab(sl, a, inv, shift_ref, pick_v, field, picked, contrib)
            return carry

        if it == 0:
            lax.fori_loop(0, 4, project, 0)
            await_signals(partners)
            halos(0, c0_ref)
            lax.fori_loop(4, 8, project, 0)
        else:
            lax.fori_loop(0, 8, project, 0)
        total = jnp.zeros((128, 256), f32)
        for g in range(4):
            rows = slice(g * 384, (g + 1) * 384)
            for part in parts(contrib[rows], 3):
                total = total + hot(sum_p[:, rows], part)
        proj[it] = total.reshape(8, 16, 256)

        for k in (4, 3, 5, 2, 6, 1, 7):
            zz = lax.rem(z + k, 8)
            send(proj.at[it, zz], sums.at[it, k - 1], send_sem.at[base], recv_sem.at[base], line[k - 1])
        drain_halos(it, recv_sem)
        smooth(angle, slab, c_ref, zlow.at[it], zhigh.at[it], ylow.at[it], yhigh.at[it], next_ref)
        drain(sums.at[it], recv_sem.at[base])
        own = proj[it, z] - meas_ref[...]
        for k in range(7):
            own = own + sums[it, k]
        misfit[it, z] = own
        for k in (4, 3, 5, 2, 6, 1, 7):
            send(misfit.at[it, z], misfit.at[it, z], send_sem.at[base + 1], recv_sem.at[base + 1], line[k - 1])
        if it == 1:
            mout_ref[mine] = own
            for k in range(1, 8):
                target = device(angle, lax.rem(x + k // 2, 4), z, lax.rem(half + k % 2, 2))
                send(misfit.at[it, z], mout_ref.at[mine], send_sem.at[16], recv_sem.at[16], target)
        drain(misfit.at[it, pl.ds(0, 7)], recv_sem.at[base + 1])

        high, low = parts(misfit[it].reshape(128, 256), 2)
        split[:128] = high
        split[128:] = low

        def give(i, carry):
            xx, hh = lax.rem(x + lax.div(i, 2), 4), lax.rem(half + lax.rem(i, 2), 2)
            sl = xx * 2 + hh
            back_slab(sl, a, shift_ref, pick_p, sum_v, split, picked, contrib, back.at[it])
            for k in range(4):
                aa = lax.rem(angle + k, 4)
                send(back.at[it, sl, aa], got.at[it, block], send_sem.at[base + 2], recv_sem.at[base + 2], device(aa, xx, z, hh))
            return carry

        lax.fori_loop(1, 8, give, 0)
        back_slab(mine, a, shift_ref, pick_p, sum_v, split, picked, contrib, back.at[it])
        for k in range(1, 4):
            aa = lax.rem(angle + k, 4)
            send(back.at[it, mine, aa], got.at[it, block], send_sem.at[base + 2], recv_sem.at[base + 2], device(aa, x, z, half))
        got[it, block] = back[it, mine, angle]
        drain(got.at[it, pl.ds(0, 31)], recv_sem.at[base + 2])
        terms = got[it].reshape(512, 256)

        if it == 0:
            new = next_ref[...].reshape(384, 256) - STEP * dot(harm_t[...], terms)
            c1_ref[...] = new.reshape(48, 8, 256)
            fields[...] = dot(harm_f[...], new).reshape(32, 2, 8, 256)
            for k in range(1, 32):
                aa, xx, hh = lax.rem(angle + k // 8, 4), lax.rem(x + k // 2, 4), lax.rem(half + k % 2, 2)
                send(
                    fields.at[(aa * 2 + hh) * 4 + xx], field1.at[mine, angle],
                    send_sem.at[base + 3], recv_sem.at[base + 3], device(aa, xx, z, hh),
                )
            field1[mine, angle] = fields[block]
            halos(1, c1_ref)
            drain(got.at[it, pl.ds(0, 31)], recv_sem.at[base + 3])
        else:
            far = lax.rem(angle + 2, 4)
            beside = angle + 1 - 2 * lax.rem(angle, 2)
            groups = ((0, 16), (16, 16), (32, 13))

            def quarter(start, size, which):
                return out_ref.at[pl.ds(start, size), :, pl.ds(pl.multiple_of(which * 8, 8), 8), :]

            for g, (start, size) in enumerate(groups):
                rows = slice(start * 8, (start + size) * 8)
                new = next_ref[start : start + size].reshape(size * 8, 256) - STEP * dot(harm_t[rows, :], terms)
                new = new.reshape(size, 8, 256)
                for zz in range(2):
                    out_ref[start : start + size, zz, pl.ds(pl.multiple_of(angle * 8, 8), 8), :] = new[:, :, zz * 128 : zz * 128 + 128]
                piece = quarter(start, size, angle)
                send(piece, piece, send_sem.at[17 + g], recv_sem.at[17 + g], (far, slab))
                send(piece, piece, send_sem.at[20 + g], recv_sem.at[20 + g], (beside, slab))
            for g, (start, size) in enumerate(groups):
                piece = quarter(start, size, far)
                drain(piece, recv_sem.at[17 + g])
                send(piece, piece, send_sem.at[23 + g], recv_sem.at[23 + g], (beside, slab))
            for g, (start, size) in enumerate(groups):
                piece = quarter(start, size, angle)
                drain(piece, recv_sem.at[20 + g])
                drain(piece, recv_sem.at[23 + g])
                for first in (17, 20, 23):
                    drain(piece, send_sem.at[first + g])
            drain(mout_ref.at[pl.ds(0, 7)], recv_sem.at[16])
            drain(mout_ref.at[pl.ds(0, 7)], send_sem.at[16])

    for it in range(2):
        base = it * 8
        drain(sums.at[it], send_sem.at[base])
        drain(misfit.at[it, pl.ds(0, 7)], send_sem.at[base + 1])
        drain(got.at[it, pl.ds(0, 31)], send_sem.at[base + 2])
        if it == 0:
            drain(got.at[it, pl.ds(0, 31)], send_sem.at[base + 3])
        drain_halos(it, send_sem)


def main(*operands):
    return pl.pallas_call(
        main_kernel,
        out_shape=(jax.ShapeDtypeStruct((45, 2, 32, 128), f32), jax.ShapeDtypeStruct((8, 16, 256), f32)),
        in_specs=[SM] + [VM] * 10,
        out_specs=(VM, VM),
        scratch_shapes=[
            pltpu.VMEM((8, 4, 2, 8, 256), f32),
            pltpu.VMEM((48, 8, 256), f32),
            pltpu.VMEM((48, 8, 256), f32),
            pltpu.VMEM((2, 8, 16, 256), f32),
            pltpu.VMEM((2, 7, 16, 256), f32),
            pltpu.VMEM((2, 8, 16, 256), f32),
            pltpu.VMEM((TS, 256), f32),
            pltpu.VMEM((8 * TS, 256), f32),
            pltpu.VMEM((256, 256), bf16),
            pltpu.VMEM((2, 8, 4, 2, 8, 256), f32),
            pltpu.VMEM((2, 32, 2, 8, 256), f32),
            pltpu.VMEM((32, 2, 8, 256), f32),
            pltpu.VMEM((2, 48, 8, 128), f32),
            pltpu.VMEM((2, 48, 8, 128), f32),
            pltpu.VMEM((2, 48, 256), f32),
            pltpu.VMEM((2, 48, 256), f32),
            pltpu.VMEM((2, 2, 48, 256), f32),
            pltpu.SemaphoreType.DMA((26,)),
            pltpu.SemaphoreType.DMA((26,)),
        ],
        compiler_params=pltpu.CompilerParams(collective_id=1, has_side_effects=True, vmem_limit_bytes=LIMIT),
        name="main",
    )(*operands)


def pick(array, index, axis):
    return lax.dynamic_index_in_dim(array, index, axis, keepdims=False)


def per_device(coefficients, harmonics, stretch, measured, tile_pixel, tile_voxel, tile_shift, tile_count):
    angle, x, z, half = position()
    field, harm_got, packs, c_own = begin(coefficients, harmonics, tile_pixel, tile_voxel, tile_shift, tile_count, measured)

    slots = pick(packs[:, :8].reshape(8, 4, 2, 256), half, 2)[:, :3, :TS]
    pixel = slots[:, 0].astype(jnp.int32)
    voxel = slots[:, 1].astype(jnp.int32)
    pixel = lax.rem(lax.div(pixel, 4), 8) * 16 + lax.div(pixel, 32) * 4 + lax.rem(pixel, 4)
    count = 8 * TS

    def compare(ids, along, wrap):
        return jnp.where(ids == lax.rem(along, wrap), 1.0, 0.0).astype(bf16)

    pick_v = compare(voxel.reshape(count, 1), jnp.arange(192)[None, :], 64)
    pick_p = compare(pixel.reshape(count, 1), jnp.arange(256)[None, :], 128)
    sum_p = compare(pixel.reshape(1, count), jnp.arange(128)[:, None], 128)
    sum_v = compare(voxel[:, None, :], jnp.arange(64)[None, :, None], 64)
    shifts = jnp.broadcast_to(slots[:, 2].reshape(count, 1), (count, 128))
    a = pick(stretch, half, 0)
    stretch2 = jnp.stack([a, 1.0 / a])
    meas = pick(packs[:, 8:].reshape(8, 2, 8, 256), half, 1)
    meas = lax.dynamic_slice_in_dim(meas, 2 * x, 2, 1)
    meas = meas.reshape(8, 2, 2, 128).transpose(0, 2, 1, 3).reshape(16, 256)
    harm = harm_got.reshape(64, 128)[:, :48]
    eye = jnp.eye(8, dtype=f32)
    harm_f = (harm[:, None, :, None] * eye[None, :, None, :]).reshape(512, 384)
    harm_t = (harm.T[:, None, :, None] * eye[None, :, None, :]).reshape(384, 512)

    updated, mout = main(stretch2, shifts, pick_v, sum_p, pick_p, sum_v, meas, field, c_own, harm_f, harm_t)
    mout = pick(mout.reshape(4, 2, 8, 2, 2, 128), x * 2 + half, 2)
    misfit = mout.transpose(1, 0, 3, 2, 4).reshape(2, 8, 256)
    return updated, misfit


def solution(mesh):
    in_specs = (
        P(None, "slab", None, None),
        P("angle", None, None),
        P("angle"),
        P("angle", None, "slab"),
        P("angle", "slab"),
        P("angle", "slab"),
        P("angle", "slab"),
        P("angle", "slab"),
    )
    out_specs = (P(None, "slab", None, None), P("angle", None, "slab"))
    return jax.shard_map(per_device, mesh=mesh, in_specs=in_specs, out_specs=out_specs, check_vma=False)
```

time: 1370 us -> 167 us (0.12)
  waiting for transfers between devices: 1050 us -> 0 us
  matrix products: 141 us -> 0 us
  Pallas kernels: 0 us -> 112 us
  other arithmetic: 104 us -> 14.3 us
  starting transfers between devices: 14.5 us -> 0 us
    reduce_scatter x2 -> x0, waiting for transfers between devices: 629 us -> none  [per_device(): lax.psum_scatter(partial_sums, 'slab', scatter_dimension=2, tiled=True)]
    all_gather x2 -> x0, waiting for transfers between devices: 295 us -> none  [per_device(): whole_misfit = lax.all_gather(misfit, 'slab', axis=2, tiled=True)]
    dot_general x38 -> x0, matrix products: 141 us -> none  [the longest x16 81.7 us: back_accumulate(): jnp.einsum('stp,tvp->tsv', picked, weights, precision=lax.Precision.HIGHEST)]
    pallas_call x0 -> x2, Pallas kernels: none -> 112 us  [the longest x1 95.8 us: main(): pl.pallas_call(main_kernel, out_shape=(jax.ShapeDtypeStruct((45, 2, 32, 1...]
    ppermute x4 -> x0, waiting for transfers between devices: 81.2 us -> none  [the longest x2 55.2 us: padded_2(): lax.ppermute(lax.slice_in_dim(block, block.shape[dim] - width, None, axis...]
    scatter-add x32 -> x0, other arithmetic: 70.3 us -> none  [the longest x16 35.2 us: back_accumulate(): return (total.at[block_voxels].add(contrib), None)]
    psum x2 -> x0, waiting for transfers between devices: 47 us -> none  [per_device(): gradient = lax.psum(local_terms, 'angle')]
    gather x32 -> x0, local copies, waits for them, and re-layouts: 19.5 us -> none  [the longest x16 9.73 us: project_accumulate(): picked = seg_field[:, block_voxels, :]]
  transfers between devices with their start and end apart: 10 -> 0, of which waited for: 10 -> 0; matrix products, arithmetic and copies ran while one was open for 0% -> 0% of each run, Pallas kernels for 0% -> 0%
where the time goes in v3:
time: 167 us; the launch traced here: 166 us
  Pallas kernels  112 us (67%)
  local copies, waits for them, and re-layouts  38.3 us (23%)
  other arithmetic  14.3 us (9%)
    pallas_call x1, Pallas kernels, main(): pl.pallas_call(main_kernel, out_shape=(jax.ShapeDtypeStruct((45, 2, 32, 1...  95.8 us
    pallas_call x1, Pallas kernels, begin(): pl.pallas_call(begin_kernel, out_shape=(jax.ShapeDtypeStruct((8, 4, 2, 8,...  16.4 us
    unnamed x31, local copies, waits for them, and re-layouts  15.2 us
    mul x1, local copies, waits for them, and re-layouts, per_device(): harm.T[:, None, :, None] * eye[None, :, None, :]  9.74 us
    mul x1, local copies, waits for them, and re-layouts, per_device(): harm_f = (harm[:, None, :, None] * eye[None, :, None, :]).reshape(512, 384)  9 us
    mul x1, other arithmetic, per_device(): harm.T[:, None, :, None] * eye[None, :, None, :]  6.19 us
    mul x1, other arithmetic, per_device(): harm_f = (harm[:, None, :, None] * eye[None, :, None, :]).reshape(512, 384)  5.4 us

profile of v3, /device:TPU:1, one launch (start us, length us, event | category | flops | bytes accessed | tf_op | source)
XLA Modules:
  0.0 166.4 jit_solution(1773981057143562460)
XLA Ops:
  0.7 1.2 dynamic_slice.17
  2.6 1.2 pad_maximum_fusion.stretch_ref
  3.8 0.7 copy.17.count_ref
  4.6 1.4 copy-done.1
  5.9 0.7 copy-done.8
  6.6 0.7 copy-done.9
  7.4 0.7 copy-done.10
  8.0 0.7 copy-done.11
  8.7 0.7 copy-done.12
  9.4 16.4 %begin.1 = (f32[8,4,2,8,256]{4,3,2,1,0:T(8,128)S(1)}, f32[4,16,128]{2,1,0:T(8,128)S(1)}, f32[8,24,256]{2,1,0:T(8,128)S(1)}, f32[48,8,256]{2,1,0:T(8,128)S(1)}) custom-call(f32[16,45]{1,0:T(8,128)S(1)} %bitcast.37, f32[45,2,32,128]{3,2,1,0:T(8,128)S(1)} %copy-done.1, f32[2,8,45]{2,1,0:T(8,128)S(1)} %copy-done.8, s32[2,192]{1,0:T(2,128)S(1)} %copy-done.10, ...), custom_call_target="tpu_custom_call" | custom-call | tf_op jit(solution)/shard_map/begin/pallas_call | solution.py:135
  25.9 0.8 copy-done.3
  26.7 0.8 copy-done.5
  27.6 0.1 convert_element_type.52
  27.9 0.8 select_convert_fusion.3.sum_v
  28.8 0.1 select_convert_fusion.2.sum_p
  28.9 0.3 select_convert_fusion.pick_p
  29.2 0.3 select_convert_fusion.1.pick_v
  29.5 1.1 broadcast_in_dim.49.shift_ref
  30.6 6.2 %broadcast_multiply_fusion = f32[48,8,64,8]{3,2,1,0:T(8,128)} fusion(f32[8,8]{1,0:T(8,128)S(1)} %fusion.6, f32[48,64]{1,0:T(8,128)S(1)} %copy.19), kind=kLoop, calls=%fused_computation | loop fusion | flops 196608 | bytes 798976 | tf_op jit(solution)/shard_map/mul | solution.py:453
  36.8 9.7 %mul.74.harm_t = f32[384,512]{1,0:T(8,128)S(1)} reshape(f32[48,8,64,8]{3,2,1,0:T(8,128)} %broadcast_multiply_fusion) | data formatting | bytes 1572864 | tf_op jit(solution)/shard_map/mul | solution.py:453
  46.5 5.4 %broadcast_multiply_fusion.1 = f32[64,8,48,8]{3,2,1,0:T(8,128)} fusion(f32[8,8]{1,0:T(8,128)S(1)} %fusion.6, f32[64,48]{1,0:T(8,128)S(1)} %get-tuple-element.15), kind=kLoop, calls=%fused_computation.1 | loop fusion | flops 196608 | bytes 798976 | tf_op jit(solution)/shard_map/mul | solution.py:452
  51.9 9.0 %mul.70.harm_f = f32[512,384]{1,0:T(8,128)S(1)} reshape(f32[64,8,48,8]{3,2,1,0:T(8,128)} %broadcast_multiply_fusion.1) | data formatting | bytes 1572864 | tf_op jit(solution)/shard_map/mul | solution.py:452
  61.0 1.1 copy-done
  62.1 0.9 copy-done.2
  63.0 1.0 copy-done.4
  64.1 1.0 copy-done.6
  65.1 0.6 copy-done.13
  65.7 95.8 %main.1 = (f32[45,2,32,128]{3,2,1,0:T(8,128)}, f32[8,16,256]{2,1,0:T(8,128)S(1)}) custom-call(f32[2]{0:T(128)S(1)} %copy-done.13, f32[1536,128]{1,0:T(8,128)S(1)} %copy-done, bf16[1536,192]{1,0:T(8,128)(2,1)S(1)} %select_convert_fusion.1.pick_v, bf16[128,1536]{1,0:T(8,128)(2,1)S(1)} %select_convert_fusion.2.sum_p, ...), custom_call_target="tpu_custom_call" | custom-call | tf_op jit(solution)/shard_map/main/pallas_call | solution.py:392
  161.5 0.6 copy-done.7
  162.1 1.0 reshape.170
  163.1 0.6 reshape.171
  163.8 2.7 %copy.29 = f32[45,2,32,128]{3,2,1,0:T(8,128)} copy(f32[45,2,32,128]{3,2,1,0:T(8,128)} %get-tuple-element.22) | data formatting | bytes 2949120
  (34 shorter events, 0.4 us)
Async XLA Ops:
  4.6 1.4 copy-start.1
  5.9 0.7 copy-start.8
  6.6 0.7 copy-start.9
  7.4 0.7 copy-start.10
  8.0 0.7 copy-start.11
  8.7 0.7 copy-start.12
  25.8 0.8 copy-start.3
  26.7 0.8 copy-start.5
  60.9 1.1 copy-start
  62.1 0.9 copy-start.2
  63.0 1.0 copy-start.4
  64.1 1.0 copy-start.6
  65.1 0.6 copy-start.13
  161.5 0.7 copy-start.7

commit v4 on v3

v4 whole, which is shorter than its diff:
```python
import jax
import jax.numpy as jnp
from jax import lax
from jax.experimental import pallas as pl
from jax.experimental.pallas import tpu as pltpu
from jax.sharding import PartitionSpec as P

f32 = jnp.float32
bf16 = jnp.bfloat16
MESH = pl.DeviceIdType.MESH
STEP = 0.003
SMOOTH = 6.0
FAR = 1.0e6
TS = 192
CHUNK = 48
TAKE = lax.GatherDimensionNumbers(
    offset_dims=(), collapsed_slice_dims=(1,), start_index_map=(1,), operand_batching_dims=(0,), start_indices_batching_dims=(0,)
)

VM = pl.BlockSpec(memory_space=pltpu.VMEM)
SM = pl.BlockSpec(memory_space=pltpu.SMEM)
LIMIT = 48 * 2**20


def position():
    angle = lax.axis_index("angle")
    slab = lax.axis_index("slab")
    return angle, lax.div(slab, 16), lax.rem(lax.div(slab, 2), 8), lax.rem(slab, 2)


def device(angle, x, z, half):
    return (angle, (x * 8 + z) * 2 + half)


def signal(partners):
    barrier = pltpu.get_barrier_semaphore()
    for partner in partners:
        pl.semaphore_signal(barrier, inc=1, device_id=partner, device_id_type=MESH)


def await_signals(partners):
    pl.semaphore_wait(pltpu.get_barrier_semaphore(), len(partners))


def send(src, dst, send_sem, recv_sem, target):
    pltpu.make_async_remote_copy(
        src_ref=src, dst_ref=dst, send_sem=send_sem, recv_sem=recv_sem, device_id=target, device_id_type=MESH
    ).start()


def drain(like, sem):
    pltpu.make_async_copy(like, like, sem).wait()


def dot(a, b):
    return jnp.dot(a, b, preferred_element_type=f32, precision=lax.Precision.HIGHEST)


def hot(a, b):
    return jnp.dot(a, b, preferred_element_type=f32)


def parts(value, count):
    found = []
    for _ in range(count - 1):
        part = value.astype(bf16)
        found.append(part)
        value = value - part.astype(f32)
    return found + [value.astype(bf16)]


def take(values, lanes):
    return lax.gather(values, lanes[..., None], TAKE, slice_sizes=(1, 1), mode=lax.GatherScatterMode.PROMISE_IN_BOUNDS)


def project_slab(i, a, inv, shift_ref, pick_ref, field, picked, contrib):
    rows = [
        jnp.concatenate([field[i, y, s, :, zz * 128 : zz * 128 + 128] for s in range(2)], axis=1)
        for zz in range(2)
        for y in range(4)
    ]
    split = jnp.concatenate(parts(jnp.concatenate(rows, axis=0), 3), axis=0)
    picked[...] = hot(pick_ref[pl.ds(pl.multiple_of(i * TS, TS), TS), :], split)
    lane = lax.broadcasted_iota(jnp.int32, (CHUNK, 128), 1).astype(f32)
    for c in range(TS // CHUNK):
        at = pl.ds(pl.multiple_of(i * TS + c * CHUNK, 16), CHUNK)
        u = lane - shift_ref[at, :]
        v0 = jnp.floor((u - 1.0) * inv) + 1.0
        t0 = u - a * v0
        first = v0.astype(jnp.int32)
        taps = (1.0 - t0, 1.0 - jnp.abs(t0 - a), 1.0 + t0 - 2.0 * a, 1.0 + t0 - 3.0 * a)
        lanes, weights = [], []
        for k in range(4):
            v = first + k
            inside = v & 127
            lanes.append(inside)
            weights.append(jnp.where(v == inside, jnp.maximum(taps[k], 0.0), 0.0))
        for s in range(2):
            f = picked[c * CHUNK : (c + 1) * CHUNK, s * 128 : s * 128 + 128]
            terms = [take(f, lanes[k]) * weights[k] for k in range(4)]
            contrib[at, s * 128 : s * 128 + 128] = (terms[0] + terms[1]) + (terms[2] + terms[3])


def back_slab(i, a, shift_ref, pick_ref, sum_ref, split, picked, contrib, back):
    picked[...] = hot(pick_ref[pl.ds(pl.multiple_of(i * TS, TS), TS), :], split[...])
    lane = lax.broadcasted_iota(jnp.int32, (CHUNK, 128), 1).astype(f32)
    for c in range(TS // CHUNK):
        at = slice(c * CHUNK, (c + 1) * CHUNK)
        t = shift_ref[pl.ds(pl.multiple_of(i * TS + c * CHUNK, 16), CHUNK), :] + a * lane
        p0 = jnp.floor(t)
        w1 = t - p0
        w0 = jnp.where(p0 <= 127.0, 1.0 - w1, 0.0)
        w1 = jnp.where(p0 <= 126.0, w1, 0.0)
        first = p0.astype(jnp.int32)
        lane0, lane1 = first & 127, (first + 1) & 127
        for s in range(2):
            m = picked[at, s * 128 : s * 128 + 128]
            contrib[at, s * 128 : s * 128 + 128] = take(m, lane0) * w0 + take(m, lane1) * w1
    high, low = parts(contrib[:TS], 2)
    total = hot(sum_ref[i], high) + hot(sum_ref[i], low)
    for y in range(4):
        for s in range(2):
            for zz in range(2):
                row = zz * 32 + y * 8
                back[i, y, s, :, zz * 128 : zz * 128 + 128] = total[row : row + 8, s * 128 : s * 128 + 128]


def smooth(angle, slab, c_ref, zlow, zhigh, ylow, yhigh, next_ref):
    lane = lax.broadcasted_iota(jnp.int32, (8, 128), 1)
    sub = lax.broadcasted_iota(jnp.int32, (8, 128), 0)
    has_zlow = (slab > 0).astype(f32)
    has_zhigh = (slab < 63).astype(f32)
    has_ylow = (angle > 0).astype(f32)
    has_yhigh = (angle < 3).astype(f32)

    def one(k, carry):
        c = c_ref[k]
        below, above = ylow[pl.ds(k, 1), :] * has_ylow, yhigh[pl.ds(k, 1), :] * has_yhigh
        half = (c[:, :128], c[:, 128:])
        deep = (zlow[k] * has_zlow + half[1], half[0] + zhigh[k] * has_zhigh)
        for zz in range(2):
            v = half[zz]
            at = slice(zz * 128, zz * 128 + 128)
            near = deep[zz]
            near += jnp.where(sub == 0, jnp.broadcast_to(below[:, at], (8, 128)), pltpu.roll(v, 1, 0))
            near += jnp.where(sub == 7, jnp.broadcast_to(above[:, at], (8, 128)), pltpu.roll(v, 7, 0))
            near += jnp.where(lane == 0, 0.0, pltpu.roll(v, 1, 1)) + jnp.where(lane == 127, 0.0, pltpu.roll(v, 127, 1))
            next_ref[k, :, at] = v - (STEP * SMOOTH) * (6.0 * v - near)
        return carry

    lax.fori_loop(0, 48, one, 0, unroll=4)


def prepare_slots(packs, half, pick_v, pick_p, sum_v, sum_p, shift_b):
    row = lax.broadcasted_iota(jnp.int32, (8, 640), 0)
    lane = lax.broadcasted_iota(jnp.int32, (8, 640), 1)
    spread = ((lane < 256) & (row == 0)) | ((lane >= 256) & (lane < 512) & (row == 1)) | ((lane >= 512) & (row >= 2) & (row <= 4))
    spread = jnp.where(spread, 1.0, 0.0).astype(bf16)
    id_v = lax.rem(lax.broadcasted_iota(jnp.int32, (TS, 192), 1), 64).astype(f32)
    id_p = lax.rem(lax.broadcasted_iota(jnp.int32, (TS, 256), 1), 128).astype(f32)
    sub_v = lax.broadcasted_iota(jnp.int32, (64, TS), 0).astype(f32)
    sub_p = lax.broadcasted_iota(jnp.int32, (128, 2 * TS), 0).astype(f32)

    def hit(ids, along):
        return jnp.where(ids == along, 1.0, 0.0).astype(bf16)

    rows_p = []
    for i in range(8):
        pixel = packs[i, pl.ds(half, 1), :]
        voxel = packs[i, pl.ds(2 + half, 1), :]
        shift = packs[i, pl.ds(4 + half, 1), :]
        split = [part.astype(f32) for part in parts(shift, 3)]
        rows = jnp.concatenate([voxel, pixel] + split + [jnp.zeros((3, 256), f32)], axis=0)
        wide = hot(rows.T.astype(bf16)[:TS], spread)
        at = slice(i * TS, (i + 1) * TS)
        pick_v[at, :] = hit(wide[:, :192], id_v)
        pick_p[at, :] = hit(wide[:, 256:512], id_p)
        shift_b[at, :] = wide[:, 512:640]
        sum_v[i] = hit(voxel[:, :TS], sub_v)
        rows_p.append(pixel[:, :TS])
    for g in range(4):
        sum_p[:, g * 384 : (g + 1) * 384] = hit(jnp.concatenate(rows_p[2 * g : 2 * g + 2], axis=1), sub_p)


def prepare_harmonics(harm_all, harm_f, harm_t):
    harm = harm_all[...].reshape(64, 128)

    def spread(rows, columns, along):
        big = lax.broadcasted_iota(jnp.int32, (rows, columns), along)
        small = lax.broadcasted_iota(jnp.int32, (rows, columns), 1 - along)
        return jnp.where(lax.div(big, 8) == small, 1.0, 0.0)

    def diagonal(rows, columns):
        r = lax.broadcasted_iota(jnp.int32, (rows, columns), 0)
        c = lax.broadcasted_iota(jnp.int32, (rows, columns), 1)
        return lax.rem(r, 8) == lax.rem(c, 8)

    wide = dot(harm, spread(128, 384, 1))
    harm_f[...] = jnp.where(diagonal(512, 384), dot(spread(512, 64, 0), wide), 0.0)
    wide = dot(harm.T, spread(64, 512, 1))
    full = jnp.where(diagonal(384, 512), dot(spread(384, 128, 0), wide), 0.0)
    high, low = parts(full, 2)
    harm_t[:, :512] = high
    harm_t[:, 512:1024] = high
    harm_t[:, 1024:] = low


SEM_PACK, SEM_HARM, SEM_FIELD, SEM_SUM, SEM_ALL, SEM_BACK, SEM_HALO, SEM_MIS, SEM_FAR, SEM_NEAR, SEM_PASS = (
    0, 1, 2, 18, 20, 22, 24, 32, 33, 36, 39,
)
SEMS = 42
FAR_FIRST = (4, 3, 5, 2, 6, 1, 7)


def kernel(
    c_hbm, harm_hbm, stretch_hbm, meas_hbm, pix_hbm, vox_hbm, shift_hbm, count_hbm,
    out_ref, mout_ref,
    c_all, harm_v, harm_s, stretch_s, meas_v, pix_v, vox_v, shift_v, count_v,
    pack, packs, blocks, field0, field1, harm_all, harm_f, harm_t, pick_v, pick_p, sum_v, sum_p, shift_b, meas_own,
    c0_ref, c1_ref, next_ref, proj, sums, misfit, picked, contrib, split, back, got, fields, zlow, zhigh, ylow, yhigh, edges,
    send_sem, recv_sem, load_sem,
):
    angle, x, z, half = position()
    slab = (x * 8 + z) * 2 + half
    mine = x * 2 + half
    block = (angle * 2 + half) * 4 + x
    plane = [
        device(lax.rem(angle + k // 8, 4), lax.rem(x + k // 2, 4), z, lax.rem(half + k % 2, 2)) for k in range(1, 32)
    ]
    line = [device(angle, x, lax.rem(z + k, 8), half) for k in range(1, 8)]
    beyond = (angle, lax.rem(slab + 2 * half + 63, 64))
    partners = plane + line + [beyond]
    above = (angle, lax.rem(slab + 1, 64))
    below = (angle, lax.rem(slab + 63, 64))
    right = (lax.rem(angle + 1, 4), slab)
    left = (lax.rem(angle + 3, 4), slab)
    back_of = [((4 - i // 2) % 4) * 2 + i % 2 for i in range(8)]

    loads = [
        pltpu.make_async_copy(src, dst, load_sem.at[n])
        for n, (src, dst) in enumerate(
            [
                (c_hbm, c_all), (harm_hbm, harm_s), (harm_hbm, harm_v), (pix_hbm, pix_v), (vox_hbm, vox_v),
                (shift_hbm, shift_v), (count_hbm, count_v), (meas_hbm, meas_v), (stretch_hbm, stretch_s),
            ]
        )
    ]
    for load in loads:
        load.start()
    signal(partners)
    for load in loads:
        load.wait()

    pixel = pix_v[...]
    pixel = lax.rem(lax.div(pixel, 4), 8) * 16 + lax.div(pixel, 32) * 4 + lax.rem(pixel, 4)
    valid = lax.broadcasted_iota(jnp.int32, (2, TS), 1) < count_v[...]
    pack[...] = jnp.zeros_like(pack)
    pack[0:2, :TS] = pixel.astype(f32)
    pack[2:4, :TS] = vox_v[...].astype(f32)
    pack[4:6, :TS] = jnp.where(valid, shift_v[...], FAR)
    pack[8:16] = meas_v[0]
    pack[16:24] = meas_v[1]
    packs[0] = pack[...]
    harm_all[angle] = jnp.zeros((16, 128), f32)
    harm_all[angle, 0:8, 0:45] = harm_v[0]
    harm_all[angle, 8:16, 0:45] = harm_v[1]
    quarter_y = pl.ds(pl.multiple_of(angle * 8, 8), 8)
    c0_ref[:45, :, 0:128] = c_all[:, 0, quarter_y, :]
    c0_ref[:45, :, 128:256] = c_all[:, 1, quarter_y, :]
    c0_ref[45:] = jnp.zeros((3, 8, 256), f32)

    def first_fields(which, segments, dest):
        for s in range(2):
            for zz in range(2):
                total = [None] * 4
                for k in range(45):
                    h = harm_s[which, segments * 2 + s, k]
                    for y in range(4):
                        term = c_all[k, zz, y * 8 : y * 8 + 8, :] * h
                        total[y] = term if k == 0 else total[y] + term
                for y in range(4):
                    dest[y, s, :, zz * 128 : zz * 128 + 128] = total[y]

    def first_block(i, carry):
        first_fields(lax.rem(half + lax.rem(i, 2), 2), lax.rem(x + lax.div(i, 2), 4), blocks.at[i])
        return carry

    lax.fori_loop(0, 8, first_block, 0)
    await_signals(partners)
    peers = [device(angle, lax.rem(x + i // 2, 4), z, lax.rem(half + i % 2, 2)) for i in range(8)]
    for i in range(1, 8):
        send(pack, packs.at[back_of[i]], send_sem.at[SEM_PACK], recv_sem.at[SEM_PACK], peers[i])
    for i in range(1, 8):
        send(
            blocks.at[i], field0.at[back_of[i]], send_sem.at[SEM_FIELD], recv_sem.at[SEM_FIELD + back_of[i]], peers[i]
        )
    for k in range(1, 4):
        target = device(lax.rem(angle + k, 4), x, z, half)
        send(harm_all.at[angle], harm_all.at[angle], send_sem.at[SEM_HARM], recv_sem.at[SEM_HARM], target)

    def halos(it, c_ref):
        at = SEM_HALO + it * 4
        edges[it, 0] = c_ref[:, 7, :]
        edges[it, 1] = c_ref[:, 0, :]
        send(c_ref.at[:, :, pl.ds(128, 128)], zlow.at[it], send_sem.at[at], recv_sem.at[at], above)
        send(c_ref.at[:, :, pl.ds(0, 128)], zhigh.at[it], send_sem.at[at + 1], recv_sem.at[at + 1], below)
        send(edges.at[it, 0], ylow.at[it], send_sem.at[at + 2], recv_sem.at[at + 2], right)
        send(edges.at[it, 1], yhigh.at[it], send_sem.at[at + 3], recv_sem.at[at + 3], left)

    def drain_halos(it, sems):
        for n, ref in enumerate((zlow, zhigh, ylow, yhigh)):
            drain(ref.at[it], sems.at[SEM_HALO + it * 4 + n])

    halos(0, c0_ref)
    field0[0] = blocks[0]
    a = stretch_s[half]
    inv = 1.0 / jnp.full((8, 128), a, f32)[0:1, :]
    drain(packs.at[pl.ds(0, 7)], recv_sem.at[SEM_PACK])
    prepare_slots(packs, half, pick_v, pick_p, sum_v, sum_p, shift_b)
    for n in range(8):
        i = lax.rem(n // 2 - x + 4, 4) * 2 + lax.rem(n % 2 - half + 2, 2)
        for s in range(2):
            line_of = packs[i, pl.ds(8 + half * 8 + x * 2 + s, 1), :]
            for tile in range(2):
                row = n * 2 + tile
                meas_own[row : row + 1, s * 128 : s * 128 + 128] = line_of[:, tile * 128 : tile * 128 + 128]

    for it in range(2):
        field = field0 if it == 0 else field1
        c_ref = c0_ref if it == 0 else c1_ref
        sem_field = SEM_FIELD + it * 8

        def project(i, carry):
            project_slab(i, a, inv, shift_b, pick_v, field, picked, contrib)

            @pl.when(i < 7)
            def _():
                drain(field.at[i + 1], recv_sem.at[sem_field + i + 1])

            return carry

        lax.fori_loop(0, 8, project, 0)
        total = jnp.zeros((128, 256), f32)
        for g in range(4):
            rows = slice(g * 384, (g + 1) * 384)
            for part in parts(contrib[rows], 3):
                total = total + hot(sum_p[:, rows], part)
        proj[it] = total.reshape(8, 16, 256)

        for k in FAR_FIRST:
            zz = lax.rem(z + k, 8)
            send(proj.at[it, zz], sums.at[it, k - 1], send_sem.at[SEM_SUM + it], recv_sem.at[SEM_SUM + it], line[k - 1])
        drain_halos(it, recv_sem)
        smooth(angle, slab, c_ref, zlow.at[it], zhigh.at[it], ylow.at[it], yhigh.at[it], next_ref)
        drain(sums.at[it], recv_sem.at[SEM_SUM + it])
        own = proj[it, z] - meas_own[...]
        for k in range(7):
            own = own + sums[it, k]
        misfit[it, z] = own
        for k in FAR_FIRST:
            send(misfit.at[it, z], misfit.at[it, z], send_sem.at[SEM_ALL + it], recv_sem.at[SEM_ALL + it], line[k - 1])
        if it == 0:
            drain(harm_all.at[pl.ds(0, 3)], recv_sem.at[SEM_HARM])
            prepare_harmonics(harm_all, harm_f, harm_t)
        else:
            mout_ref[mine] = own
            for i in range(1, 8):
                send(misfit.at[it, z], mout_ref.at[mine], send_sem.at[SEM_MIS], recv_sem.at[SEM_MIS], peers[i])
        drain(misfit.at[it, pl.ds(0, 7)], recv_sem.at[SEM_ALL + it])

        high, low = parts(misfit[it].reshape(128, 256), 2)
        split[:128] = high
        split[128:] = low

        def give(i, carry):
            xx, hh = lax.rem(x + lax.div(i, 2), 4), lax.rem(half + lax.rem(i, 2), 2)
            back_slab(i, a, shift_b, pick_p, sum_v, split, picked, contrib, back.at[it])
            for k in range(4):
                aa = lax.rem(angle + k, 4)
                send(
                    back.at[it, i, aa], got.at[it, block],
                    send_sem.at[SEM_BACK + it], recv_sem.at[SEM_BACK + it], device(aa, xx, z, hh),
                )
            return carry

        lax.fori_loop(1, 8, give, 0)
        back_slab(0, a, shift_b, pick_p, sum_v, split, picked, contrib, back.at[it])
        for k in range(1, 4):
            aa = lax.rem(angle + k, 4)
            send(
                back.at[it, 0, aa], got.at[it, block],
                send_sem.at[SEM_BACK + it], recv_sem.at[SEM_BACK + it], device(aa, x, z, half),
            )
        got[it, block] = back[it, 0, angle]
        drain(got.at[it, pl.ds(0, 31)], recv_sem.at[SEM_BACK + it])
        high, low = parts(got[it].reshape(512, 256), 2)
        terms = jnp.concatenate([high, low, high], axis=0)

        if it == 0:
            new = next_ref[...].reshape(384, 256) - STEP * hot(harm_t[...], terms)
            c1_ref[...] = new.reshape(48, 8, 256)
            fields[...] = dot(harm_f[...], new).reshape(32, 2, 8, 256)
            for k in sorted(range(1, 32), key=lambda k: (k % 8, k)):
                aa, xx, hh = lax.rem(angle + k // 8, 4), lax.rem(x + k % 8 // 2, 4), lax.rem(half + k % 2, 2)
                to = back_of[k % 8]
                send(
                    fields.at[(aa * 2 + hh) * 4 + xx], field1.at[to, angle],
                    send_sem.at[SEM_FIELD + 8], recv_sem.at[SEM_FIELD + 8 + to], device(aa, xx, z, hh),
                )
            field1[0, angle] = fields[block]
            halos(1, c1_ref)
            drain(field1.at[0, pl.ds(0, 3)], recv_sem.at[SEM_FIELD + 8])
        else:
            far = lax.rem(angle + 2, 4)
            beside = angle + 1 - 2 * lax.rem(angle, 2)
            groups = ((0, 16), (16, 16), (32, 13))

            def quarter(start, size, which):
                return out_ref.at[pl.ds(start, size), :, pl.ds(pl.multiple_of(which * 8, 8), 8), :]

            for g, (start, size) in enumerate(groups):
                rows = slice(start * 8, (start + 16) * 8)
                new = next_ref[start : start + 16].reshape(128, 256) - STEP * hot(harm_t[rows, :], terms)
                new = new.reshape(16, 8, 256)[:size]
                for zz in range(2):
                    out_ref[start : start + size, zz, quarter_y, :] = new[:, :, zz * 128 : zz * 128 + 128]
                piece = quarter(start, size, angle)
                send(piece, piece, send_sem.at[SEM_FAR + g], recv_sem.at[SEM_FAR + g], (far, slab))
                send(piece, piece, send_sem.at[SEM_NEAR + g], recv_sem.at[SEM_NEAR + g], (beside, slab))
            for g, (start, size) in enumerate(groups):
                piece = quarter(start, size, far)
                drain(piece, recv_sem.at[SEM_FAR + g])
                send(piece, piece, send_sem.at[SEM_PASS + g], recv_sem.at[SEM_PASS + g], (beside, slab))
            for g, (start, size) in enumerate(groups):
                piece = quarter(start, size, angle)
                drain(piece, recv_sem.at[SEM_NEAR + g])
                drain(piece, recv_sem.at[SEM_PASS + g])
                for first in (SEM_FAR, SEM_NEAR, SEM_PASS):
                    drain(piece, send_sem.at[first + g])
            drain(mout_ref.at[pl.ds(0, 7)], recv_sem.at[SEM_MIS])
            drain(mout_ref.at[pl.ds(0, 7)], send_sem.at[SEM_MIS])

    drain(packs.at[pl.ds(0, 7)], send_sem.at[SEM_PACK])
    drain(harm_all.at[pl.ds(0, 3)], send_sem.at[SEM_HARM])
    drain(field0.at[pl.ds(0, 7)], send_sem.at[SEM_FIELD])
    drain(got.at[0, pl.ds(0, 31)], send_sem.at[SEM_FIELD + 8])
    for it in range(2):
        drain(sums.at[it], send_sem.at[SEM_SUM + it])
        drain(misfit.at[it, pl.ds(0, 7)], send_sem.at[SEM_ALL + it])
        drain(got.at[it, pl.ds(0, 31)], send_sem.at[SEM_BACK + it])
        drain_halos(it, send_sem)


def per_device(coefficients, harmonics, stretch, measured, tile_pixel, tile_voxel, tile_shift, tile_count):
    angle, x, z, half = position()
    operands = (coefficients, harmonics, stretch, measured, tile_pixel, tile_voxel, tile_shift, tile_count)
    scratch = [
        pltpu.VMEM((45, 2, 32, 128), f32),
        pltpu.VMEM((2, 8, 45), f32),
        pltpu.SMEM((2, 8, 45), f32),
        pltpu.SMEM((2,), f32),
        pltpu.VMEM((2, 8, 256), f32),
        pltpu.VMEM((2, TS), jnp.int32),
        pltpu.VMEM((2, TS), jnp.int32),
        pltpu.VMEM((2, TS), f32),
        pltpu.VMEM((2, 1), jnp.int32),
        pltpu.VMEM((24, 256), f32),
        pltpu.VMEM((8, 24, 256), f32),
        pltpu.VMEM((8, 4, 2, 8, 256), f32),
        pltpu.VMEM((8, 4, 2, 8, 256), f32),
        pltpu.VMEM((8, 4, 2, 8, 256), f32),
        pltpu.VMEM((4, 16, 128), f32),
        pltpu.VMEM((512, 384), f32),
        pltpu.VMEM((384, 1536), bf16),
        pltpu.VMEM((8 * TS, 192), bf16),
        pltpu.VMEM((8 * TS, 256), bf16),
        pltpu.VMEM((8, 64, TS), bf16),
        pltpu.VMEM((128, 8 * TS), bf16),
        pltpu.VMEM((8 * TS, 128), f32),
        pltpu.VMEM((16, 256), f32),
        pltpu.VMEM((48, 8, 256), f32),
        pltpu.VMEM((48, 8, 256), f32),
        pltpu.VMEM((48, 8, 256), f32),
        pltpu.VMEM((2, 8, 16, 256), f32),
        pltpu.VMEM((2, 7, 16, 256), f32),
        pltpu.VMEM((2, 8, 16, 256), f32),
        pltpu.VMEM((TS, 256), f32),
        pltpu.VMEM((8 * TS, 256), f32),
        pltpu.VMEM((256, 256), bf16),
        pltpu.VMEM((2, 8, 4, 2, 8, 256), f32),
        pltpu.VMEM((2, 32, 2, 8, 256), f32),
        pltpu.VMEM((32, 2, 8, 256), f32),
        pltpu.VMEM((2, 48, 8, 128), f32),
        pltpu.VMEM((2, 48, 8, 128), f32),
        pltpu.VMEM((2, 48, 256), f32),
        pltpu.VMEM((2, 48, 256), f32),
        pltpu.VMEM((2, 2, 48, 256), f32),
        pltpu.SemaphoreType.DMA((SEMS,)),
        pltpu.SemaphoreType.DMA((SEMS,)),
        pltpu.SemaphoreType.DMA((9,)),
    ]
    updated, mout = pl.pallas_call(
        kernel,
        out_shape=(jax.ShapeDtypeStruct((45, 2, 32, 128), f32), jax.ShapeDtypeStruct((8, 16, 256), f32)),
        in_specs=[pl.BlockSpec(memory_space=pl.ANY)] * 8,
        out_specs=(VM, VM),
        scratch_shapes=scratch,
        compiler_params=pltpu.CompilerParams(collective_id=0, has_side_effects=True, vmem_limit_bytes=LIMIT),
        name="tomography",
    )(*operands)
    mout = lax.dynamic_index_in_dim(mout.reshape(4, 2, 8, 2, 2, 128), x * 2 + half, 2, keepdims=False)
    misfit = mout.transpose(1, 0, 3, 2, 4).reshape(2, 8, 256)
    return updated, misfit


def solution(mesh):
    in_specs = (
        P(None, "slab", None, None),
        P("angle", None, None),
        P("angle"),
        P("angle", None, "slab"),
        P("angle", "slab"),
        P("angle", "slab"),
        P("angle", "slab"),
        P("angle", "slab"),
    )
    out_specs = (P(None, "slab", None, None), P("angle", None, "slab"))
    return jax.shard_map(per_device, mesh=mesh, in_specs=in_specs, out_specs=out_specs, check_vma=False)
```

time: 167 us -> 116 us (0.69)
  local copies, waits for them, and re-layouts: 38.3 us -> 8.05 us
  other arithmetic: 14.3 us -> 0 us
  Pallas kernels: 112 us -> 107 us
    mul x2 -> x0, local copies, waits for them, and re-layouts: 18.7 us -> none  [the longest x1 9.74 us: per_device(): harm.T[:, None, :, None] * eye[None, :, None, :]]
    mul x2 -> x0, other arithmetic: 11.6 us -> none  [the longest x1 6.19 us: per_device(): harm.T[:, None, :, None] * eye[None, :, None, :]]
    unnamed x31 -> x16, local copies, waits for them, and re-layouts: 15.2 us -> 7.34 us
    pallas_call x2 -> x1, Pallas kernels: 112 us -> 107 us  [per_device(): pl.pallas_call(kernel, out_shape=(jax.ShapeDtypeStruct((45, 2, 32, 128),...]
where the time goes in v4:
time: 116 us
  Pallas kernels  107 us (92%)
  local copies, waits for them, and re-layouts  8.05 us (7%)
    pallas_call x1, Pallas kernels, per_device(): pl.pallas_call(kernel, out_shape=(jax.ShapeDtypeStruct((45, 2, 32, 128),...  107 us
    unnamed x16, local copies, waits for them, and re-layouts  7.34 us

profile of v4, /device:TPU:1, one launch (start us, length us, event | category | flops | bytes accessed | tf_op | source)
XLA Modules:
  0.0 115.9 jit_solution(17638513593889952094)
XLA Ops:
  0.6 0.7 copy.13.count_hbm
  1.4 0.0 copy-start
  1.4 1.4 %copy-done = f32[45,2,32,128]{3,2,1,0:T(8,128)S(1)} copy-done((f32[45,2,32,128]{3,2,1,0:T(8,128)S(1)}, f32[45,2,32,128]{3,2,1,0:T(8,128)}, u32[]{:S(2)}) %copy-start) | copy-done | bytes 1474584
  2.8 0.0 copy-start.1
  2.8 0.7 copy-done.1
  3.5 0.0 copy-start.2
  3.5 0.7 copy-done.2
  4.2 0.0 copy-start.3
  4.2 0.7 copy-done.3
  4.9 0.0 copy-start.4
  4.9 0.7 copy-done.4
  5.5 0.0 copy-start.5
  5.5 0.7 copy-done.5
  6.2 0.0 copy-start.6
  6.2 0.7 copy-done.6
  6.9 107.1 %tomography.1 = (f32[45,2,32,128]{3,2,1,0:T(8,128)S(1)}, f32[8,16,256]{2,1,0:T(8,128)S(1)}) custom-call(f32[45,2,32,128]{3,2,1,0:T(8,128)S(1)} %copy-done, f32[2,8,45]{2,1,0:T(8,128)S(1)} %copy-done.2, f32[2]{0:T(128)S(1)} %copy-done.6, f32[2,8,256]{2,1,0:T(8,128)S(1)} %copy-done.1, s32[2,192]{1,0:T(2,128)S(1)} %copy-done.3, s32[2,192]{1,0:T(2,128)S(1)} %copy-done.4, ...), custom_call_target="tpu_custom_call" | custom-call | tf_op jit(solution)/shard_map/tomography/pallas_call | solution.py:502
  114.0 0.1 reshape.10
  114.1 0.6 reshape.11
  114.7 1.1 copy.18
  (2 shorter events, 0.0 us)
Async XLA Ops:
  1.4 1.4 %copy-start = (f32[45,2,32,128]{3,2,1,0:T(8,128)S(1)}, f32[45,2,32,128]{3,2,1,0:T(8,128)}, u32[]{:S(2)}) copy-start(f32[45,2,32,128]{3,2,1,0:T(8,128)} %c_hbm.1) | copy-start | bytes 4423684
  2.8 0.7 copy-start.1
  3.5 0.7 copy-start.2
  4.2 0.7 copy-start.3
  4.9 0.7 copy-start.4
  5.5 0.7 copy-start.5
  6.2 0.7 copy-start.6

commit v5 on v4

--- a/solution.py
+++ b/solution.py
@@ -10,7 +10,8 @@
 MESH = pl.DeviceIdType.MESH
 STEP = 0.003
 SMOOTH = 6.0
-FAR = 1.0e6
+FAR = 128.0
+FIX = 23
 TS = 192
 CHUNK = 48
 TAKE = lax.GatherDimensionNumbers(
@@ -19,7 +20,7 @@
 
 VM = pl.BlockSpec(memory_space=pltpu.VMEM)
 SM = pl.BlockSpec(memory_space=pltpu.SMEM)
-LIMIT = 48 * 2**20
+LIMIT = 56 * 2**20
 
 
 def position():
@@ -73,40 +74,92 @@
     return lax.gather(values, lanes[..., None], TAKE, slice_sizes=(1, 1), mode=lax.GatherScatterMode.PROMISE_IN_BOUNDS)
 
 
-def project_slab(i, a, inv, shift_ref, pick_ref, field, picked, contrib):
+def project_pick(i, pick_ref, field, picked):
     rows = [
         jnp.concatenate([field[i, y, s, :, zz * 128 : zz * 128 + 128] for s in range(2)], axis=1)
         for zz in range(2)
         for y in range(4)
     ]
-    split = jnp.concatenate(parts(jnp.concatenate(rows, axis=0), 3), axis=0)
+    rows = jnp.concatenate(rows, axis=0)
+    ahead = [pltpu.roll(rows[:, s * 128 : s * 128 + 128], 127, 1) for s in range(2)]
+    split = jnp.concatenate(parts(jnp.concatenate([rows] + ahead, axis=1), 3), axis=0)
     picked[...] = hot(pick_ref[pl.ds(pl.multiple_of(i * TS, TS), TS), :], split)
-    lane = lax.broadcasted_iota(jnp.int32, (CHUNK, 128), 1).astype(f32)
-    for c in range(TS // CHUNK):
-        at = pl.ds(pl.multiple_of(i * TS + c * CHUNK, 16), CHUNK)
-        u = lane - shift_ref[at, :]
-        v0 = jnp.floor((u - 1.0) * inv) + 1.0
-        t0 = u - a * v0
-        first = v0.astype(jnp.int32)
-        taps = (1.0 - t0, 1.0 - jnp.abs(t0 - a), 1.0 + t0 - 2.0 * a, 1.0 + t0 - 3.0 * a)
-        lanes, weights = [], []
-        for k in range(4):
-            v = first + k
-            inside = v & 127
-            lanes.append(inside)
-            weights.append(jnp.where(v == inside, jnp.maximum(taps[k], 0.0), 0.0))
-        for s in range(2):
-            f = picked[c * CHUNK : (c + 1) * CHUNK, s * 128 : s * 128 + 128]
-            terms = [take(f, lanes[k]) * weights[k] for k in range(4)]
-            contrib[at, s * 128 : s * 128 + 128] = (terms[0] + terms[1]) + (terms[2] + terms[3])
-
-
-def back_slab(i, a, shift_ref, pick_ref, sum_ref, split, picked, contrib, back):
-    picked[...] = hot(pick_ref[pl.ds(pl.multiple_of(i * TS, TS), TS), :], split[...])
-    lane = lax.broadcasted_iota(jnp.int32, (CHUNK, 128), 1).astype(f32)
+
+
+def project_slots(i, stretch, shift_ref, picked, contrib):
+    one = 1 << FIX
+    scale = 1.0 / one
+    lane = lax.broadcasted_iota(jnp.int32, (1, 128), 1)
+    step = (jnp.full((1, 128), stretch, f32) * one + 0.5).astype(jnp.int32)
+    inverse = 1.0 / step.astype(f32)
+    steps = step * lane
+
+    def first_of(distance):
+        first = jnp.ceil(distance.astype(f32) * inverse - 2.0e-4).astype(jnp.int32)
+        first = jnp.where(first * step < distance, first + 1, first)
+        return jnp.maximum(first, 0)
+
     for c in range(TS // CHUNK):
         at = slice(c * CHUNK, (c + 1) * CHUNK)
-        t = shift_ref[pl.ds(pl.multiple_of(i * TS + c * CHUNK, 16), CHUNK), :] + a * lane
+        start = (shift_ref[pl.ds(pl.multiple_of(i * TS + c * CHUNK, 16), CHUNK), :] * one + 0.5).astype(jnp.int32)
+        here = start + steps
+        after = here + step
+        w1 = (here & (one - 1)).astype(f32) * scale
+        w0 = 1.0 - w1
+        both = (lax.shift_right_arithmetic(here, FIX) == lax.shift_right_arithmetic(after, FIX)) & (lane < 127)
+        next1 = (after & (one - 1)).astype(f32) * scale
+        next0 = jnp.where(both, 1.0 - next1, 0.0)
+        next1 = jnp.where(both, next1, 0.0)
+        distance = (lane << FIX) - start
+        first0, first1 = first_of(distance), first_of(distance - one)
+        has0 = (first0 <= 127) & (distance > -one)
+        has1 = (first1 <= 127) & (distance > 0)
+        first0, first1 = first0 & 127, first1 & 127
+        for s in range(2):
+            f = picked[at, s * 128 : s * 128 + 128]
+            g = picked[at, 256 + s * 128 : 256 + s * 128 + 128]
+            low = jnp.where(has0, take(w0 * f + next0 * g, first0), 0.0)
+            high = jnp.where(has1, take(w1 * f + next1 * g, first1), 0.0)
+            contrib[at, s * 128 : s * 128 + 128] = low + high
+
+
+def project_sum(i, sum_ref, contrib, total):
+    for part in parts(contrib[...], 3):
+        total[...] += hot(sum_ref[i], part)
+
+
+def project_all(stretch, shift_ref, pick_ref, sum_ref, field, arrived, rows, added, total):
+    total[...] = jnp.zeros_like(total)
+
+    def step(i, odd, pick_next=True, sum_last=True):
+        if pick_next:
+            arrived(i + 1)
+            project_pick(i + 1, pick_ref, field, rows[1 - odd])
+        project_slots(i, stretch, shift_ref, rows[odd], added[odd])
+        if sum_last:
+            project_sum(i - 1, sum_ref, added[1 - odd], total)
+
+    def pair(p, carry):
+        step(2 * p + 1, 1)
+        step(2 * p + 2, 0)
+        return carry
+
+    project_pick(0, pick_ref, field, rows[0])
+    step(0, 0, sum_last=False)
+    lax.fori_loop(0, 3, pair, 0)
+    step(7, 1, pick_next=False)
+    project_sum(7, sum_ref, added[1], total)
+
+
+def back_pick(i, pick_ref, split, picked):
+    picked[:, :256] = hot(pick_ref[pl.ds(pl.multiple_of(i * TS, TS), TS), :], split[...])
+
+
+def back_slots(i, stretch, shift_ref, picked, contrib):
+    lane = lax.broadcasted_iota(jnp.int32, (1, 128), 1).astype(f32) * stretch
+    for c in range(TS // CHUNK):
+        at = slice(c * CHUNK, (c + 1) * CHUNK)
+        t = shift_ref[pl.ds(pl.multiple_of(i * TS + c * CHUNK, 16), CHUNK), :] + lane
         p0 = jnp.floor(t)
         w1 = t - p0
         w0 = jnp.where(p0 <= 127.0, 1.0 - w1, 0.0)
@@ -116,13 +169,37 @@
         for s in range(2):
             m = picked[at, s * 128 : s * 128 + 128]
             contrib[at, s * 128 : s * 128 + 128] = take(m, lane0) * w0 + take(m, lane1) * w1
-    high, low = parts(contrib[:TS], 2)
+
+
+def back_sum(i, sum_ref, contrib, back):
+    high, low = parts(contrib[...], 2)
     total = hot(sum_ref[i], high) + hot(sum_ref[i], low)
     for y in range(4):
         for s in range(2):
             for zz in range(2):
                 row = zz * 32 + y * 8
                 back[i, y, s, :, zz * 128 : zz * 128 + 128] = total[row : row + 8, s * 128 : s * 128 + 128]
+
+
+def back_all(stretch, shift_ref, pick_ref, sum_ref, split, give, rows, added, back):
+    def step(i, odd, pick_next=True, sum_last=True):
+        if pick_next:
+            back_pick(lax.rem(i + 1, 8), pick_ref, split, rows[1 - odd])
+        back_slots(lax.rem(i, 8), stretch, shift_ref, rows[odd], added[odd])
+        if sum_last:
+            back_sum(i - 1, sum_ref, added[1 - odd], back)
+            give(i - 1)
+
+    def pair(p, carry):
+        step(2 * p + 2, 0)
+        step(2 * p + 3, 1)
+        return carry
+
+    back_pick(1, pick_ref, split, rows[1])
+    step(1, 1, sum_last=False)
+    lax.fori_loop(0, 3, pair, 0)
+    step(8, 0, pick_next=False)
+    back_sum(0, sum_ref, added[0], back)
 
 
 def smooth(angle, slab, c_ref, zlow, zhigh, ylow, yhigh, next_ref):
@@ -159,12 +236,11 @@
     id_v = lax.rem(lax.broadcasted_iota(jnp.int32, (TS, 192), 1), 64).astype(f32)
     id_p = lax.rem(lax.broadcasted_iota(jnp.int32, (TS, 256), 1), 128).astype(f32)
     sub_v = lax.broadcasted_iota(jnp.int32, (64, TS), 0).astype(f32)
-    sub_p = lax.broadcasted_iota(jnp.int32, (128, 2 * TS), 0).astype(f32)
+    sub_p = lax.broadcasted_iota(jnp.int32, (128, TS), 0).astype(f32)
 
     def hit(ids, along):
         return jnp.where(ids == along, 1.0, 0.0).astype(bf16)
 
-    rows_p = []
     for i in range(8):
         pixel = packs[i, pl.ds(half, 1), :]
         voxel = packs[i, pl.ds(2 + half, 1), :]
@@ -177,9 +253,7 @@
         pick_p[at, :] = hit(wide[:, 256:512], id_p)
         shift_b[at, :] = wide[:, 512:640]
         sum_v[i] = hit(voxel[:, :TS], sub_v)
-        rows_p.append(pixel[:, :TS])
-    for g in range(4):
-        sum_p[:, g * 384 : (g + 1) * 384] = hit(jnp.concatenate(rows_p[2 * g : 2 * g + 2], axis=1), sub_p)
+        sum_p[i] = hit(pixel[:, :TS], sub_p)
 
 
 def prepare_harmonics(harm_all, harm_f, harm_t):
@@ -215,9 +289,9 @@
 def kernel(
     c_hbm, harm_hbm, stretch_hbm, meas_hbm, pix_hbm, vox_hbm, shift_hbm, count_hbm,
     out_ref, mout_ref,
-    c_all, harm_v, harm_s, stretch_s, meas_v, pix_v, vox_v, shift_v, count_v,
+    c_all, harm_v, harm_s, stretch_s, meas_v, pix_v, vox_v, shift_v, count_s,
     pack, packs, blocks, field0, field1, harm_all, harm_f, harm_t, pick_v, pick_p, sum_v, sum_p, shift_b, meas_own,
-    c0_ref, c1_ref, next_ref, proj, sums, misfit, picked, contrib, split, back, got, fields, zlow, zhigh, ylow, yhigh, edges,
+    c0_ref, c1_ref, next_ref, proj, sums, misfit, rows_a, rows_b, added_a, added_b, total, split, back, got, fields, zlow, zhigh, ylow, yhigh, edges,
     send_sem, recv_sem, load_sem,
 ):
     angle, x, z, half = position()
@@ -241,7 +315,7 @@
         for n, (src, dst) in enumerate(
             [
                 (c_hbm, c_all), (harm_hbm, harm_s), (harm_hbm, harm_v), (pix_hbm, pix_v), (vox_hbm, vox_v),
-                (shift_hbm, shift_v), (count_hbm, count_v), (meas_hbm, meas_v), (stretch_hbm, stretch_s),
+                (shift_hbm, shift_v), (count_hbm, count_s), (meas_hbm, meas_v), (stretch_hbm, stretch_s),
             ]
         )
     ]
@@ -253,7 +327,8 @@
 
     pixel = pix_v[...]
     pixel = lax.rem(lax.div(pixel, 4), 8) * 16 + lax.div(pixel, 32) * 4 + lax.rem(pixel, 4)
-    valid = lax.broadcasted_iota(jnp.int32, (2, TS), 1) < count_v[...]
+    first = lax.broadcasted_iota(jnp.int32, (2, TS), 0) == 0
+    valid = lax.broadcasted_iota(jnp.int32, (2, TS), 1) < jnp.where(first, count_s[0, 0], count_s[0, 1])
     pack[...] = jnp.zeros_like(pack)
     pack[0:2, :TS] = pixel.astype(f32)
     pack[2:4, :TS] = vox_v[...].astype(f32)
@@ -311,10 +386,8 @@
         for n, ref in enumerate((zlow, zhigh, ylow, yhigh)):
             drain(ref.at[it], sems.at[SEM_HALO + it * 4 + n])
 
-    halos(0, c0_ref)
     field0[0] = blocks[0]
     a = stretch_s[half]
-    inv = 1.0 / jnp.full((8, 128), a, f32)[0:1, :]
     drain(packs.at[pl.ds(0, 7)], recv_sem.at[SEM_PACK])
     prepare_slots(packs, half, pick_v, pick_p, sum_v, sum_p, shift_b)
     for n in range(8):
@@ -330,28 +403,15 @@
         c_ref = c0_ref if it == 0 else c1_ref
         sem_field = SEM_FIELD + it * 8
 
-        def project(i, carry):
-            project_slab(i, a, inv, shift_b, pick_v, field, picked, contrib)
-
-            @pl.when(i < 7)
-            def _():
-                drain(field.at[i + 1], recv_sem.at[sem_field + i + 1])
-
-            return carry
-
-        lax.fori_loop(0, 8, project, 0)
-        total = jnp.zeros((128, 256), f32)
-        for g in range(4):
-            rows = slice(g * 384, (g + 1) * 384)
-            for part in parts(contrib[rows], 3):
-                total = total + hot(sum_p[:, rows], part)
-        proj[it] = total.reshape(8, 16, 256)
+        def arrived(i):
+            drain(field.at[i], recv_sem.at[sem_field + i])
+
+        project_all(a, shift_b, pick_v, sum_p, field, arrived, (rows_a, rows_b), (added_a, added_b), total)
+        proj[it] = total[...].reshape(8, 16, 256)
 
         for k in FAR_FIRST:
             zz = lax.rem(z + k, 8)
             send(proj.at[it, zz], sums.at[it, k - 1], send_sem.at[SEM_SUM + it], recv_sem.at[SEM_SUM + it], line[k - 1])
-        drain_halos(it, recv_sem)
-        smooth(angle, slab, c_ref, zlow.at[it], zhigh.at[it], ylow.at[it], yhigh.at[it], next_ref)
         drain(sums.at[it], recv_sem.at[SEM_SUM + it])
         own = proj[it, z] - meas_own[...]
         for k in range(7):
@@ -359,6 +419,7 @@
         misfit[it, z] = own
         for k in FAR_FIRST:
             send(misfit.at[it, z], misfit.at[it, z], send_sem.at[SEM_ALL + it], recv_sem.at[SEM_ALL + it], line[k - 1])
+        halos(it, c_ref)
         if it == 0:
             drain(harm_all.at[pl.ds(0, 3)], recv_sem.at[SEM_HARM])
             prepare_harmonics(harm_all, harm_f, harm_t)
@@ -372,19 +433,16 @@
         split[:128] = high
         split[128:] = low
 
-        def give(i, carry):
+        def give(i):
             xx, hh = lax.rem(x + lax.div(i, 2), 4), lax.rem(half + lax.rem(i, 2), 2)
-            back_slab(i, a, shift_b, pick_p, sum_v, split, picked, contrib, back.at[it])
             for k in range(4):
                 aa = lax.rem(angle + k, 4)
                 send(
                     back.at[it, i, aa], got.at[it, block],
                     send_sem.at[SEM_BACK + it], recv_sem.at[SEM_BACK + it], device(aa, xx, z, hh),
                 )
-            return carry
-
-        lax.fori_loop(1, 8, give, 0)
-        back_slab(0, a, shift_b, pick_p, sum_v, split, picked, contrib, back.at[it])
+
+        back_all(a, shift_b, pick_p, sum_v, split, give, (rows_a, rows_b), (added_a, added_b), back.at[it])
         for k in range(1, 4):
             aa = lax.rem(angle + k, 4)
             send(
@@ -392,6 +450,8 @@
                 send_sem.at[SEM_BACK + it], recv_sem.at[SEM_BACK + it], device(aa, x, z, half),
             )
         got[it, block] = back[it, 0, angle]
+        drain_halos(it, recv_sem)
+        smooth(angle, slab, c_ref, zlow.at[it], zhigh.at[it], ylow.at[it], yhigh.at[it], next_ref)
         drain(got.at[it, pl.ds(0, 31)], recv_sem.at[SEM_BACK + it])
         high, low = parts(got[it].reshape(512, 256), 2)
         terms = jnp.concatenate([high, low, high], axis=0)
@@ -408,7 +468,6 @@
                     send_sem.at[SEM_FIELD + 8], recv_sem.at[SEM_FIELD + 8 + to], device(aa, xx, z, hh),
                 )
             field1[0, angle] = fields[block]
-            halos(1, c1_ref)
             drain(field1.at[0, pl.ds(0, 3)], recv_sem.at[SEM_FIELD + 8])
         else:
             far = lax.rem(angle + 2, 4)
@@ -453,7 +512,7 @@
 
 def per_device(coefficients, harmonics, stretch, measured, tile_pixel, tile_voxel, tile_shift, tile_count):
     angle, x, z, half = position()
-    operands = (coefficients, harmonics, stretch, measured, tile_pixel, tile_voxel, tile_shift, tile_count)
+    operands = (coefficients, harmonics, stretch, measured, tile_pixel, tile_voxel, tile_shift, tile_count.T)
     scratch = [
         pltpu.VMEM((45, 2, 32, 128), f32),
         pltpu.VMEM((2, 8, 45), f32),
@@ -463,7 +522,7 @@
         pltpu.VMEM((2, TS), jnp.int32),
         pltpu.VMEM((2, TS), jnp.int32),
         pltpu.VMEM((2, TS), f32),
-        pltpu.VMEM((2, 1), jnp.int32),
+        pltpu.SMEM((1, 2), jnp.int32),
         pltpu.VMEM((24, 256), f32),
         pltpu.VMEM((8, 24, 256), f32),
         pltpu.VMEM((8, 4, 2, 8, 256), f32),
@@ -475,7 +534,7 @@
         pltpu.VMEM((8 * TS, 192), bf16),
         pltpu.VMEM((8 * TS, 256), bf16),
         pltpu.VMEM((8, 64, TS), bf16),
-        pltpu.VMEM((128, 8 * TS), bf16),
+        pltpu.VMEM((8, 128, TS), bf16),
         pltpu.VMEM((8 * TS, 128), f32),
         pltpu.VMEM((16, 256), f32),
         pltpu.VMEM((48, 8, 256), f32),
@@ -484,8 +543,11 @@
         pltpu.VMEM((2, 8, 16, 256), f32),
         pltpu.VMEM((2, 7, 16, 256), f32),
         pltpu.VMEM((2, 8, 16, 256), f32),
+        pltpu.VMEM((TS, 512), f32),
+        pltpu.VMEM((TS, 512), f32),
         pltpu.VMEM((TS, 256), f32),
-        pltpu.VMEM((8 * TS, 256), f32),
+        pltpu.VMEM((TS, 256), f32),
+        pltpu.VMEM((128, 256), f32),
         pltpu.VMEM((256, 256), bf16),
         pltpu.VMEM((2, 8, 4, 2, 8, 256), f32),
         pltpu.VMEM((2, 32, 2, 8, 256), f32),
@@ -502,7 +564,7 @@
     updated, mout = pl.pallas_call(
         kernel,
         out_shape=(jax.ShapeDtypeStruct((45, 2, 32, 128), f32), jax.ShapeDtypeStruct((8, 16, 256), f32)),
-        in_specs=[pl.BlockSpec(memory_space=pl.ANY)] * 8,
+        in_specs=[pl.BlockSpec(memory_space=pltpu.HBM)] * 8,
         out_specs=(VM, VM),
         scratch_shapes=scratch,
         compiler_params=pltpu.CompilerParams(collective_id=0, has_side_effects=True, vmem_limit_bytes=LIMIT),

time: 116 us -> 103 us (0.89)
  Pallas kernels: 107 us -> 97.9 us
  local copies, waits for them, and re-layouts: 8.05 us -> 4.29 us
    pallas_call x1, Pallas kernels: 107 us -> 97.9 us  [per_device(): pl.pallas_call(kernel, out_shape=(jax.ShapeDtypeStruct((45, 2, 32, 128),...]
    unnamed x16 -> x1, local copies, waits for them, and re-layouts: 7.34 us -> 2.68 us
where the time goes in v5:
time: 103 us
  Pallas kernels  97.9 us (95%)
  local copies, waits for them, and re-layouts  4.29 us (4%)
    pallas_call x1, Pallas kernels, per_device(): pl.pallas_call(kernel, out_shape=(jax.ShapeDtypeStruct((45, 2, 32, 128),...  97.9 us
    unnamed x1, local copies, waits for them, and re-layouts  2.68 us

profile of v5, /device:TPU:1, one launch (start us, length us, event | category | flops | bytes accessed | tf_op | source)
XLA Modules:
  0.0 102.8 jit_solution(10428812458064987349)
XLA Ops:
  0.6 97.9 %tomography.1 = (f32[45,2,32,128]{3,2,1,0:T(8,128)}, f32[8,16,256]{2,1,0:T(8,128)}) custom-call(f32[45,2,32,128]{3,2,1,0:T(8,128)} %c_hbm.1, f32[2,8,45]{2,1,0:T(8,128)} %harm_hbm.1, f32[2]{0:T(128)} %stretch_hbm.1, f32[2,8,256]{2,1,0:T(8,128)} %meas_hbm.1, s32[2,192]{1,0:T(2,128)} %pix_hbm.1, s32[2,192]{1,0:T(2,128)} %vox_hbm.1, f32[2,192]{1,0:T(2,128)} %shift_hbm.1, ...), custom_call_target="tpu_custom_call" | custom-call | tf_op jit(solution)/shard_map/tomography/pallas_call | solution.py:564
  98.5 1.0 reshape.10
  99.5 0.6 reshape.11
  100.2 2.7 %copy.15 = f32[45,2,32,128]{3,2,1,0:T(8,128)} copy(f32[45,2,32,128]{3,2,1,0:T(8,128)} %get-tuple-element.8) | data formatting | bytes 2949120
  (2 shorter events, 0.0 us)

commit v6 on v5

--- a/solution.py
+++ b/solution.py
@@ -83,7 +83,7 @@
     rows = jnp.concatenate(rows, axis=0)
     ahead = [pltpu.roll(rows[:, s * 128 : s * 128 + 128], 127, 1) for s in range(2)]
     split = jnp.concatenate(parts(jnp.concatenate([rows] + ahead, axis=1), 3), axis=0)
-    picked[...] = hot(pick_ref[pl.ds(pl.multiple_of(i * TS, TS), TS), :], split)
+    picked[...] = hot(pick_ref[slice(i * TS, (i + 1) * TS), :], split)
 
 
 def project_slots(i, stretch, shift_ref, picked, contrib):
@@ -101,7 +101,7 @@
 
     for c in range(TS // CHUNK):
         at = slice(c * CHUNK, (c + 1) * CHUNK)
-        start = (shift_ref[pl.ds(pl.multiple_of(i * TS + c * CHUNK, 16), CHUNK), :] * one + 0.5).astype(jnp.int32)
+        start = (shift_ref[slice(i * TS + c * CHUNK, i * TS + (c + 1) * CHUNK), :] * one + 0.5).astype(jnp.int32)
         here = start + steps
         after = here + step
         w1 = (here & (one - 1)).astype(f32) * scale
@@ -131,35 +131,29 @@
 def project_all(stretch, shift_ref, pick_ref, sum_ref, field, arrived, rows, added, total):
     total[...] = jnp.zeros_like(total)
 
-    def step(i, odd, pick_next=True, sum_last=True):
-        if pick_next:
-            arrived(i + 1)
-            project_pick(i + 1, pick_ref, field, rows[1 - odd])
-        project_slots(i, stretch, shift_ref, rows[odd], added[odd])
-        if sum_last:
-            project_sum(i - 1, sum_ref, added[1 - odd], total)
-
-    def pair(p, carry):
-        step(2 * p + 1, 1)
-        step(2 * p + 2, 0)
-        return carry
-
-    project_pick(0, pick_ref, field, rows[0])
-    step(0, 0, sum_last=False)
-    lax.fori_loop(0, 3, pair, 0)
-    step(7, 1, pick_next=False)
-    project_sum(7, sum_ref, added[1], total)
+    def step(n, odd):
+        if n < 7:
+            arrived(ARRIVE[n + 1])
+            project_pick(ARRIVE[n + 1], pick_ref, field, rows[1 - odd])
+        project_slots(ARRIVE[n], stretch, shift_ref, rows[odd], added[odd])
+        if n > 0:
+            project_sum(ARRIVE[n - 1], sum_ref, added[1 - odd], total)
+
+    project_pick(ARRIVE[0], pick_ref, field, rows[0])
+    for n in range(8):
+        step(n, n % 2)
+    project_sum(ARRIVE[7], sum_ref, added[1], total)
 
 
 def back_pick(i, pick_ref, split, picked):
-    picked[:, :256] = hot(pick_ref[pl.ds(pl.multiple_of(i * TS, TS), TS), :], split[...])
+    picked[:, :256] = hot(pick_ref[slice(i * TS, (i + 1) * TS), :], split[...])
 
 
 def back_slots(i, stretch, shift_ref, picked, contrib):
     lane = lax.broadcasted_iota(jnp.int32, (1, 128), 1).astype(f32) * stretch
     for c in range(TS // CHUNK):
         at = slice(c * CHUNK, (c + 1) * CHUNK)
-        t = shift_ref[pl.ds(pl.multiple_of(i * TS + c * CHUNK, 16), CHUNK), :] + lane
+        t = shift_ref[slice(i * TS + c * CHUNK, i * TS + (c + 1) * CHUNK), :] + lane
         p0 = jnp.floor(t)
         w1 = t - p0
         w0 = jnp.where(p0 <= 127.0, 1.0 - w1, 0.0)
@@ -182,24 +176,16 @@
 
 
 def back_all(stretch, shift_ref, pick_ref, sum_ref, split, give, rows, added, back):
-    def step(i, odd, pick_next=True, sum_last=True):
-        if pick_next:
-            back_pick(lax.rem(i + 1, 8), pick_ref, split, rows[1 - odd])
-        back_slots(lax.rem(i, 8), stretch, shift_ref, rows[odd], added[odd])
-        if sum_last:
-            back_sum(i - 1, sum_ref, added[1 - odd], back)
-            give(i - 1)
-
-    def pair(p, carry):
-        step(2 * p + 2, 0)
-        step(2 * p + 3, 1)
-        return carry
-
-    back_pick(1, pick_ref, split, rows[1])
-    step(1, 1, sum_last=False)
-    lax.fori_loop(0, 3, pair, 0)
-    step(8, 0, pick_next=False)
-    back_sum(0, sum_ref, added[0], back)
+    back_pick(DEPART[0], pick_ref, split, rows[0])
+    for n in range(8):
+        odd = n % 2
+        if n < 7:
+            back_pick(DEPART[n + 1], pick_ref, split, rows[1 - odd])
+        back_slots(DEPART[n], stretch, shift_ref, rows[odd], added[odd])
+        if n > 0:
+            back_sum(DEPART[n - 1], sum_ref, added[1 - odd], back)
+            give(DEPART[n - 1])
+    back_sum(DEPART[7], sum_ref, added[1], back)
 
 
 def smooth(angle, slab, c_ref, zlow, zhigh, ylow, yhigh, next_ref):
@@ -280,18 +266,20 @@
 
 
 SEM_PACK, SEM_HARM, SEM_FIELD, SEM_SUM, SEM_ALL, SEM_BACK, SEM_HALO, SEM_MIS, SEM_FAR, SEM_NEAR, SEM_PASS = (
-    0, 1, 2, 18, 20, 22, 24, 32, 33, 36, 39,
+    0, 1, 2, 18, 20, 22, 24, 32, 33, 37, 41,
 )
-SEMS = 42
+SEMS = 45
 FAR_FIRST = (4, 3, 5, 2, 6, 1, 7)
+ARRIVE = (0, 5, 3, 7, 4, 1, 2, 6)
+DEPART = (5, 3, 7, 4, 1, 2, 6, 0)
 
 
 def kernel(
     c_hbm, harm_hbm, stretch_hbm, meas_hbm, pix_hbm, vox_hbm, shift_hbm, count_hbm,
-    out_ref, mout_ref,
+    out_ref, mis_ref,
     c_all, harm_v, harm_s, stretch_s, meas_v, pix_v, vox_v, shift_v, count_s,
     pack, packs, blocks, field0, field1, harm_all, harm_f, harm_t, pick_v, pick_p, sum_v, sum_p, shift_b, meas_own,
-    c0_ref, c1_ref, next_ref, proj, sums, misfit, rows_a, rows_b, added_a, added_b, total, split, back, got, fields, zlow, zhigh, ylow, yhigh, edges,
+    c0_ref, c1_ref, next_ref, proj, sums, misfit, rows_a, rows_b, added_a, added_b, total, split, back, got, fields, deep, ylow, yhigh, edges, mine_out, mine_got,
     send_sem, recv_sem, load_sem,
 ):
     angle, x, z, half = position()
@@ -304,8 +292,6 @@
     line = [device(angle, x, lax.rem(z + k, 8), half) for k in range(1, 8)]
     beyond = (angle, lax.rem(slab + 2 * half + 63, 64))
     partners = plane + line + [beyond]
-    above = (angle, lax.rem(slab + 1, 64))
-    below = (angle, lax.rem(slab + 63, 64))
     right = (lax.rem(angle + 1, 4), slab)
     left = (lax.rem(angle + 3, 4), slab)
     back_of = [((4 - i // 2) % 4) * 2 + i % 2 for i in range(8)]
@@ -322,7 +308,7 @@
     for load in loads:
         load.start()
     signal(partners)
-    for load in loads:
+    for load in loads[1:]:
         load.wait()
 
     pixel = pix_v[...]
@@ -340,9 +326,14 @@
     harm_all[angle, 0:8, 0:45] = harm_v[0]
     harm_all[angle, 8:16, 0:45] = harm_v[1]
     quarter_y = pl.ds(pl.multiple_of(angle * 8, 8), 8)
-    c0_ref[:45, :, 0:128] = c_all[:, 0, quarter_y, :]
-    c0_ref[:45, :, 128:256] = c_all[:, 1, quarter_y, :]
-    c0_ref[45:] = jnp.zeros((3, 8, 256), f32)
+    await_signals(partners)
+    peers = [device(angle, lax.rem(x + i // 2, 4), z, lax.rem(half + i % 2, 2)) for i in range(8)]
+    for i in range(1, 8):
+        send(pack, packs.at[back_of[i]], send_sem.at[SEM_PACK], recv_sem.at[SEM_PACK], peers[i])
+    for k in range(1, 4):
+        target = device(lax.rem(angle + k, 4), x, z, half)
+        send(harm_all.at[angle], harm_all.at[angle], send_sem.at[SEM_HARM], recv_sem.at[SEM_HARM], target)
+    loads[0].wait()
 
     def first_fields(which, segments, dest):
         for s in range(2):
@@ -356,37 +347,35 @@
                 for y in range(4):
                     dest[y, s, :, zz * 128 : zz * 128 + 128] = total[y]
 
-    def first_block(i, carry):
-        first_fields(lax.rem(half + lax.rem(i, 2), 2), lax.rem(x + lax.div(i, 2), 4), blocks.at[i])
-        return carry
-
-    lax.fori_loop(0, 8, first_block, 0)
-    await_signals(partners)
-    peers = [device(angle, lax.rem(x + i // 2, 4), z, lax.rem(half + i % 2, 2)) for i in range(8)]
-    for i in range(1, 8):
-        send(pack, packs.at[back_of[i]], send_sem.at[SEM_PACK], recv_sem.at[SEM_PACK], peers[i])
-    for i in range(1, 8):
-        send(
-            blocks.at[i], field0.at[back_of[i]], send_sem.at[SEM_FIELD], recv_sem.at[SEM_FIELD + back_of[i]], peers[i]
-        )
-    for k in range(1, 4):
-        target = device(lax.rem(angle + k, 4), x, z, half)
-        send(harm_all.at[angle], harm_all.at[angle], send_sem.at[SEM_HARM], recv_sem.at[SEM_HARM], target)
-
-    def halos(it, c_ref):
+    for i in DEPART:
+        first_fields(lax.rem(half + i % 2, 2), lax.rem(x + i // 2, 4), blocks.at[i])
+        if i > 0:
+            send(
+                blocks.at[i], field0.at[back_of[i]], send_sem.at[SEM_FIELD], recv_sem.at[SEM_FIELD + back_of[i]], peers[i]
+            )
+    field0[0] = blocks[0]
+    c0_ref[:45, :, 0:128] = c_all[:, 0, quarter_y, :]
+    c0_ref[:45, :, 128:256] = c_all[:, 1, quarter_y, :]
+    c0_ref[45:] = jnp.zeros((3, 8, 256), f32)
+
+    def halos_beside(it, c_ref):
         at = SEM_HALO + it * 4
         edges[it, 0] = c_ref[:, 7, :]
         edges[it, 1] = c_ref[:, 0, :]
-        send(c_ref.at[:, :, pl.ds(128, 128)], zlow.at[it], send_sem.at[at], recv_sem.at[at], above)
-        send(c_ref.at[:, :, pl.ds(0, 128)], zhigh.at[it], send_sem.at[at + 1], recv_sem.at[at + 1], below)
+        src = c_ref.at[:, :, pl.ds(pl.multiple_of((1 - half) * 128, 128), 128)]
+        send(src, deep.at[it, half], send_sem.at[at], recv_sem.at[at], device(angle, x, z, 1 - half))
         send(edges.at[it, 0], ylow.at[it], send_sem.at[at + 2], recv_sem.at[at + 2], right)
         send(edges.at[it, 1], yhigh.at[it], send_sem.at[at + 3], recv_sem.at[at + 3], left)
 
+    def halos_beyond(it, c_ref):
+        at = SEM_HALO + it * 4 + 1
+        src = c_ref.at[:, :, pl.ds(pl.multiple_of(half * 128, 128), 128)]
+        send(src, deep.at[it, 1 - half], send_sem.at[at], recv_sem.at[at], beyond)
+
     def drain_halos(it, sems):
-        for n, ref in enumerate((zlow, zhigh, ylow, yhigh)):
-            drain(ref.at[it], sems.at[SEM_HALO + it * 4 + n])
-
-    field0[0] = blocks[0]
+        for n, ref in enumerate((deep.at[it, 0], deep.at[it, 1], ylow.at[it], yhigh.at[it])):
+            drain(ref, sems.at[SEM_HALO + it * 4 + n])
+
     a = stretch_s[half]
     drain(packs.at[pl.ds(0, 7)], recv_sem.at[SEM_PACK])
     prepare_slots(packs, half, pick_v, pick_p, sum_v, sum_p, shift_b)
@@ -412,6 +401,7 @@
         for k in FAR_FIRST:
             zz = lax.rem(z + k, 8)
             send(proj.at[it, zz], sums.at[it, k - 1], send_sem.at[SEM_SUM + it], recv_sem.at[SEM_SUM + it], line[k - 1])
+        halos_beside(it, c_ref)
         drain(sums.at[it], recv_sem.at[SEM_SUM + it])
         own = proj[it, z] - meas_own[...]
         for k in range(7):
@@ -419,14 +409,18 @@
         misfit[it, z] = own
         for k in FAR_FIRST:
             send(misfit.at[it, z], misfit.at[it, z], send_sem.at[SEM_ALL + it], recv_sem.at[SEM_ALL + it], line[k - 1])
-        halos(it, c_ref)
+        halos_beyond(it, c_ref)
         if it == 0:
             drain(harm_all.at[pl.ds(0, 3)], recv_sem.at[SEM_HARM])
             prepare_harmonics(harm_all, harm_f, harm_t)
         else:
-            mout_ref[mine] = own
+            mine_out[...] = jnp.zeros_like(mine_out)
+            for n in range(8):
+                mine_out[n, 0:2] = own[2 * n : 2 * n + 2]
             for i in range(1, 8):
-                send(misfit.at[it, z], mout_ref.at[mine], send_sem.at[SEM_MIS], recv_sem.at[SEM_MIS], peers[i])
+                there = lax.rem(x + i // 2, 4) * 2 + lax.rem(half + i % 2, 2)
+                send(mine_out.at[there], mine_got.at[mine], send_sem.at[SEM_MIS], recv_sem.at[SEM_MIS], peers[i])
+            mine_got[mine] = mine_out[mine]
         drain(misfit.at[it, pl.ds(0, 7)], recv_sem.at[SEM_ALL + it])
 
         high, low = parts(misfit[it].reshape(128, 256), 2)
@@ -434,7 +428,7 @@
         split[128:] = low
 
         def give(i):
-            xx, hh = lax.rem(x + lax.div(i, 2), 4), lax.rem(half + lax.rem(i, 2), 2)
+            xx, hh = lax.rem(x + i // 2, 4), lax.rem(half + i % 2, 2)
             for k in range(4):
                 aa = lax.rem(angle + k, 4)
                 send(
@@ -451,7 +445,7 @@
             )
         got[it, block] = back[it, 0, angle]
         drain_halos(it, recv_sem)
-        smooth(angle, slab, c_ref, zlow.at[it], zhigh.at[it], ylow.at[it], yhigh.at[it], next_ref)
+        smooth(angle, slab, c_ref, deep.at[it, 0], deep.at[it, 1], ylow.at[it], yhigh.at[it], next_ref)
         drain(got.at[it, pl.ds(0, 31)], recv_sem.at[SEM_BACK + it])
         high, low = parts(got[it].reshape(512, 256), 2)
         terms = jnp.concatenate([high, low, high], axis=0)
@@ -460,7 +454,7 @@
             new = next_ref[...].reshape(384, 256) - STEP * hot(harm_t[...], terms)
             c1_ref[...] = new.reshape(48, 8, 256)
             fields[...] = dot(harm_f[...], new).reshape(32, 2, 8, 256)
-            for k in sorted(range(1, 32), key=lambda k: (k % 8, k)):
+            for k in sorted(range(1, 32), key=lambda k: ARRIVE.index(k % 8)):
                 aa, xx, hh = lax.rem(angle + k // 8, 4), lax.rem(x + k % 8 // 2, 4), lax.rem(half + k % 2, 2)
                 to = back_of[k % 8]
                 send(
@@ -472,15 +466,16 @@
         else:
             far = lax.rem(angle + 2, 4)
             beside = angle + 1 - 2 * lax.rem(angle, 2)
-            groups = ((0, 16), (16, 16), (32, 13))
+            groups = ((0, 16), (16, 16), (32, 8), (40, 5))
 
             def quarter(start, size, which):
                 return out_ref.at[pl.ds(start, size), :, pl.ds(pl.multiple_of(which * 8, 8), 8), :]
 
             for g, (start, size) in enumerate(groups):
-                rows = slice(start * 8, (start + 16) * 8)
-                new = next_ref[start : start + 16].reshape(128, 256) - STEP * hot(harm_t[rows, :], terms)
-                new = new.reshape(16, 8, 256)[:size]
+                span = 16 if start < 32 else 8
+                rows = slice(start * 8, (start + span) * 8)
+                new = next_ref[start : start + span].reshape(span * 8, 256) - STEP * hot(harm_t[rows, :], terms)
+                new = new.reshape(span, 8, 256)[:size]
                 for zz in range(2):
                     out_ref[start : start + size, zz, quarter_y, :] = new[:, :, zz * 128 : zz * 128 + 128]
                 piece = quarter(start, size, angle)
@@ -496,8 +491,15 @@
                 drain(piece, recv_sem.at[SEM_PASS + g])
                 for first in (SEM_FAR, SEM_NEAR, SEM_PASS):
                     drain(piece, send_sem.at[first + g])
-            drain(mout_ref.at[pl.ds(0, 7)], recv_sem.at[SEM_MIS])
-            drain(mout_ref.at[pl.ds(0, 7)], send_sem.at[SEM_MIS])
+            drain(mine_got.at[pl.ds(0, 7)], recv_sem.at[SEM_MIS])
+            drain(mine_out.at[pl.ds(0, 7)], send_sem.at[SEM_MIS])
+            for n in range(8):
+                for s in range(2):
+                    for tile in range(2):
+                        row = n // 2 * 2 + s
+                        mis_ref[n % 2, row : row + 1, tile * 128 : tile * 128 + 128] = mine_got[
+                            n, tile : tile + 1, s * 128 : s * 128 + 128
+                        ]
 
     drain(packs.at[pl.ds(0, 7)], send_sem.at[SEM_PACK])
     drain(harm_all.at[pl.ds(0, 3)], send_sem.at[SEM_HARM])
@@ -510,8 +512,38 @@
         drain_halos(it, send_sem)
 
 
+def place_kernel(updated, misfit, updated_out, misfit_out, held, held_misfit, sem_in, sem_out):
+    pieces = [(updated.at[pl.ds(n * 5, 5)], held.at[pl.ds(n * 5, 5)], updated_out.at[pl.ds(n * 5, 5)]) for n in range(9)]
+    pieces.append((misfit, held_misfit, misfit_out))
+    into = [pltpu.make_async_copy(src, mid, sem_in.at[n]) for n, (src, mid, _) in enumerate(pieces)]
+    out = [pltpu.make_async_copy(mid, dst, sem_out.at[n]) for n, (_, mid, dst) in enumerate(pieces)]
+    for copy in into:
+        copy.start()
+    for first, second in zip(into, out):
+        first.wait()
+        second.start()
+    for copy in out:
+        copy.wait()
+
+
+def place(updated, misfit):
+    return pl.pallas_call(
+        place_kernel,
+        out_shape=(jax.ShapeDtypeStruct(updated.shape, f32), jax.ShapeDtypeStruct(misfit.shape, f32)),
+        in_specs=[pl.BlockSpec(memory_space=pltpu.HBM)] * 2,
+        out_specs=(pl.BlockSpec(memory_space=pltpu.HBM),) * 2,
+        scratch_shapes=[
+            pltpu.VMEM(updated.shape, f32),
+            pltpu.VMEM(misfit.shape, f32),
+            pltpu.SemaphoreType.DMA((10,)),
+            pltpu.SemaphoreType.DMA((10,)),
+        ],
+        compiler_params=pltpu.CompilerParams(vmem_limit_bytes=LIMIT),
+        name="place",
+    )(updated, misfit)
+
+
 def per_device(coefficients, harmonics, stretch, measured, tile_pixel, tile_voxel, tile_shift, tile_count):
-    angle, x, z, half = position()
     operands = (coefficients, harmonics, stretch, measured, tile_pixel, tile_voxel, tile_shift, tile_count.T)
     scratch = [
         pltpu.VMEM((45, 2, 32, 128), f32),
@@ -552,27 +584,26 @@
         pltpu.VMEM((2, 8, 4, 2, 8, 256), f32),
         pltpu.VMEM((2, 32, 2, 8, 256), f32),
         pltpu.VMEM((32, 2, 8, 256), f32),
-        pltpu.VMEM((2, 48, 8, 128), f32),
-        pltpu.VMEM((2, 48, 8, 128), f32),
+        pltpu.VMEM((2, 2, 48, 8, 128), f32),
         pltpu.VMEM((2, 48, 256), f32),
         pltpu.VMEM((2, 48, 256), f32),
         pltpu.VMEM((2, 2, 48, 256), f32),
+        pltpu.VMEM((8, 8, 256), f32),
+        pltpu.VMEM((8, 8, 256), f32),
         pltpu.SemaphoreType.DMA((SEMS,)),
         pltpu.SemaphoreType.DMA((SEMS,)),
         pltpu.SemaphoreType.DMA((9,)),
     ]
-    updated, mout = pl.pallas_call(
+    updated, misfit = pl.pallas_call(
         kernel,
-        out_shape=(jax.ShapeDtypeStruct((45, 2, 32, 128), f32), jax.ShapeDtypeStruct((8, 16, 256), f32)),
+        out_shape=(jax.ShapeDtypeStruct((45, 2, 32, 128), f32), jax.ShapeDtypeStruct((2, 8, 256), f32)),
         in_specs=[pl.BlockSpec(memory_space=pltpu.HBM)] * 8,
         out_specs=(VM, VM),
         scratch_shapes=scratch,
         compiler_params=pltpu.CompilerParams(collective_id=0, has_side_effects=True, vmem_limit_bytes=LIMIT),
         name="tomography",
     )(*operands)
-    mout = lax.dynamic_index_in_dim(mout.reshape(4, 2, 8, 2, 2, 128), x * 2 + half, 2, keepdims=False)
-    misfit = mout.transpose(1, 0, 3, 2, 4).reshape(2, 8, 256)
-    return updated, misfit
+    return place(updated, misfit)
 
 
 def solution(mesh):

time: 103 us -> 95.5 us (0.927)
  local copies, waits for them, and re-layouts: 4.29 us -> 0 us
  Pallas kernels: 97.9 us -> 94.6 us
    pallas_call x1, Pallas kernels: 97.9 us -> 92.3 us  [per_device(): pl.pallas_call(kernel, out_shape=(jax.ShapeDtypeStruct((45, 2, 32, 128),...]
    unnamed x1 -> x0, local copies, waits for them, and re-layouts: 2.68 us -> none
    pallas_call x0 -> x1, Pallas kernels: none -> 2.3 us  [place(): pl.pallas_call(place_kernel, out_shape=(jax.ShapeDtypeStruct(updated.shap...]
    reshape x2 -> x0, local copies, waits for them, and re-layouts: 1.59 us -> none  [the longest x1 0.97 us: per_device(): mout.reshape(4, 2, 8, 2, 2, 128)]
where the time goes in v6:
time: 95.5 us; the launch traced here: 95.4 us
  Pallas kernels  94.6 us (99%)
    pallas_call x1, Pallas kernels, per_device(): pl.pallas_call(kernel, out_shape=(jax.ShapeDtypeStruct((45, 2, 32, 128),...  92.3 us
    pallas_call x1, Pallas kernels, place(): pl.pallas_call(place_kernel, out_shape=(jax.ShapeDtypeStruct(updated.shap...  2.3 us

profile of v6, /device:TPU:1, one launch (start us, length us, event | category | flops | bytes accessed | tf_op | source)
XLA Modules:
  0.0 95.4 jit_solution(18280071177732023089)
XLA Ops:
  0.6 92.3 %tomography.1 = (f32[45,2,32,128]{3,2,1,0:T(8,128)}, f32[2,8,256]{2,1,0:T(8,128)}) custom-call(f32[45,2,32,128]{3,2,1,0:T(8,128)} %c_hbm.1, f32[2,8,45]{2,1,0:T(8,128)} %harm_hbm.1, f32[2]{0:T(128)} %stretch_hbm.1, f32[2,8,256]{2,1,0:T(8,128)} %meas_hbm.1, s32[2,192]{1,0:T(2,128)} %pix_hbm.1, s32[2,192]{1,0:T(2,128)} %vox_hbm.1, f32[2,192]{1,0:T(2,128)} %shift_hbm.1, ...), custom_call_target="tpu_custom_call" | custom-call | tf_op jit(solution)/shard_map/tomography/pallas_call | solution.py:597
  92.9 2.3 %place.1 = (f32[45,2,32,128]{3,2,1,0:T(8,128)}, f32[2,8,256]{2,1,0:T(8,128)}) custom-call(f32[45,2,32,128]{3,2,1,0:T(8,128)} %get-tuple-element.4.updated, f32[2,8,256]{2,1,0:T(8,128)} %get-tuple-element.5.misfit), custom_call_target="tpu_custom_call" | custom-call | tf_op jit(solution)/shard_map/place/pallas_call | solution.py:530
